TPU v7x, 256 devices: a whole 4x4x8 slice. The times are simulated.
256 devices in a mesh: bal: 32 (over x, z), seq: 8 (over y, core).
Axes of the slice: x: 4, y: 4, z: 8, core: 2. Of those that a mesh axis runs over, the one named last changes fastest.
Arguments:
- tokens: bfloat16 [512, 64, 5120], P('bal', 'seq'), may hold values from -6 to 6
- w_qkv: bfloat16 [5120, 24, 384], P('bal', 'seq')
- q_gain: float32 [24, 128], P('seq')
- k_gain: float32 [24, 128], P('seq')
- modulation: float32 [32, 4, 2, 5120], P('bal'), may hold values from -3 to 3
- tile_owner: int32 [512], P('bal'), may hold values from 0 to 31, as said below
- clip_dims: int32 [32, 4, 3], P('bal'), may hold values from 0 to 4, as said below
Outputs:
- attn_out: bfloat16 [512, 64, 3072], P('bal', 'seq')
Inputs may be any that keep to these rules, and one draw needn't show every extreme that they name: `tile_owner`: each owner is named by exactly 16 tiles. The 16 tiles of one bal index name any owner at most 1 times, and in every draw some owner exactly 1 times. `clip_dims`: for each owner the clips' products f h w add up to 16; entries after its last clip are 0; a clip spans at most 2 tile frames, 3 tile rows and 4 tile columns and has 4 tiles or more.
All inputs are finite; a program needn't handle non-finite values.
Results may differ from a plain program's by a relative error of at most 0.006.
Values may be sent and summed in bfloat16 or wider, within the bound.
A program may use at most 128 MiB of HBM per device.

v0:
```python
import jax
import jax.numpy as jnp
from jax import lax
from jax.sharding import PartitionSpec as P

HEADS = 24
TILES_OWN = 16


eps_norm = 1e-06
score_fill = -1e30


def tile_layout(clip_shape):
    frames_of = clip_shape[:, 0]
    rows_of = clip_shape[:, 1]
    cols_of = clip_shape[:, 2]
    clip_sizes = frames_of * rows_of * cols_of
    clip_ends = jnp.cumsum(clip_sizes)
    clip_starts = clip_ends - clip_sizes
    local_index = jnp.arange(TILES_OWN, dtype=jnp.int32)
    member = jnp.sum((local_index[:, None] >= clip_ends[None, :]).astype(jnp.int32), axis=1)
    onehot = member[:, None] == jnp.arange(clip_shape.shape[0], dtype=jnp.int32)[None, :]

    def select_clip(values):
        return jnp.sum(jnp.where(onehot, values[None, :], 0), axis=1)

    offset = local_index - select_clip(clip_starts)
    height = jnp.maximum(select_clip(rows_of), 1)
    width_tiles = jnp.maximum(select_clip(cols_of), 1)
    frame_index = offset // (height * width_tiles)
    row_index = offset // width_tiles % height
    column = offset % width_tiles

    def within_one(coords):
        return jnp.abs(coords[:, None] - coords[None, :]) <= 1

    tile_mask = (
        (member[:, None] == member[None, :])
        & within_one(frame_index)
        & within_one(row_index)
        & within_one(column)
    )
    return (onehot, tile_mask)


def clip_rows(onehot, mod_table):
    picked = jnp.sum(jnp.where(onehot[:, :, None, None], mod_table[None], 0.0), axis=1)
    return (picked[:, 0], picked[:, 1])


def modulate(pieces, shift_rows, scale_rows):
    values = pieces.astype(jnp.float32)
    center = jnp.mean(values, axis=-1, keepdims=True)
    spread = jnp.mean(jnp.square(values - center), axis=-1, keepdims=True)
    normal = (values - center) * lax.rsqrt(spread + eps_norm)
    return (normal * (1.0 + scale_rows[:, None, :]) + shift_rows[:, None, :]).astype(jnp.bfloat16)


def attend(q_block, key_rows, values, block_mask):
    scores = jnp.einsum(
        "qhd,khd->hqk", q_block, key_rows, preferred_element_type=jnp.float32
    ) * key_rows.shape[2] ** (-0.5)
    scores = jnp.where(block_mask[None], scores, score_fill)
    largest = jnp.max(scores, axis=-1, keepdims=True)
    exp_scores = jnp.exp(scores - largest)
    totals = jnp.sum(exp_scores, axis=-1, keepdims=True)
    weights = (exp_scores / totals).astype(jnp.bfloat16)
    return jnp.einsum("hqk,khd->qhd", weights, values, preferred_element_type=jnp.float32)


def per_device(tokens, w_qkv, q_gain, k_gain, modulation, tile_owner, clip_dims):
    groups = lax.axis_size("bal")
    owned_tiles, piece_len, width_model = tokens.shape
    capacity = owned_tiles // min(groups, owned_tiles)
    slot_count = groups * capacity
    flat_weight = w_qkv.reshape(w_qkv.shape[0], -1)
    slot_ids = jnp.arange(slot_count, dtype=jnp.int32)
    earlier = jnp.arange(owned_tiles)[:, None] > jnp.arange(owned_tiles)[None, :]
    slot_rank = jnp.sum((tile_owner[:, None] == tile_owner[None, :]) & earlier, axis=1)
    target = tile_owner * capacity + slot_rank
    route_onehot = (slot_ids[:, None] == target[None, :]).astype(jnp.bfloat16)
    outbound = jnp.dot(
        route_onehot, tokens.reshape(owned_tiles, -1), preferred_element_type=jnp.float32
    ).astype(jnp.bfloat16)
    outbound = outbound.reshape(groups, capacity, piece_len, width_model)
    filled = jnp.sum(route_onehot, axis=1).reshape(groups, capacity)
    arrived, arrived_flags = (
        lax.all_to_all(outbound, "bal", split_axis=0, concat_axis=0, tiled=True),
        lax.all_to_all(filled, "bal", split_axis=0, concat_axis=0, tiled=True),
    )
    live_slots = arrived_flags.reshape(slot_count) > 0.5
    position = jnp.cumsum(live_slots.astype(jnp.int32)) - 1
    collect = ((jnp.arange(TILES_OWN)[:, None] == position[None, :]) & live_slots[None, :]).astype(
        jnp.bfloat16
    )
    compact = jnp.dot(
        collect, arrived.reshape(slot_count, -1), preferred_element_type=jnp.float32
    ).astype(jnp.bfloat16)
    compact = compact.reshape(TILES_OWN, piece_len, width_model)
    onehot, tile_mask = tile_layout(clip_dims[0])
    shift_rows, scale_rows = clip_rows(onehot, modulation[0])
    whole_tiles = lax.all_gather(compact, "seq", axis=1, tiled=True)
    normed = modulate(whole_tiles, shift_rows, scale_rows)
    tile_len = normed.shape[1]
    token_rows = normed.reshape(-1, width_model)
    total_tokens = token_rows.shape[0]
    per_dev_heads = q_gain.shape[0]
    projected = jnp.dot(
        token_rows,
        lax.all_gather(flat_weight, "bal", axis=0, tiled=True),
        preferred_element_type=jnp.float32,
    )
    projected = projected.reshape(total_tokens, per_dev_heads, 3, -1)
    query = projected[:, :, 0]
    keyed = projected[:, :, 1]
    valued = projected[:, :, 2].astype(jnp.bfloat16)
    sums_q, sums_k = lax.psum(
        (jnp.sum(jnp.square(query), axis=(1, 2)), jnp.sum(jnp.square(keyed), axis=(1, 2))), "seq"
    )
    features = HEADS * query.shape[2]
    q_normed = (
        query * lax.rsqrt(sums_q / features + eps_norm)[:, None, None] * q_gain[None]
    ).astype(jnp.bfloat16)
    k_normed = (
        keyed * lax.rsqrt(sums_k / features + eps_norm)[:, None, None] * k_gain[None]
    ).astype(jnp.bfloat16)
    token_mask = jnp.repeat(jnp.repeat(tile_mask, tile_len, axis=0), tile_len, axis=1)
    block_rows = min(512, total_tokens)
    outputs = []
    for block_start in range(0, total_tokens, block_rows):
        outputs.append(
            attend(
                q_normed[block_start : block_start + block_rows],
                k_normed,
                valued,
                token_mask[block_start : block_start + block_rows],
            )
        )
    attended = jnp.concatenate(outputs, axis=0).astype(jnp.bfloat16)
    head_major = attended.reshape(TILES_OWN, tile_len, -1)
    per_token = lax.all_to_all(head_major, "seq", split_axis=1, concat_axis=2, tiled=True)
    spread_back = jnp.dot(
        collect.T, per_token.reshape(TILES_OWN, -1), preferred_element_type=jnp.float32
    ).astype(jnp.bfloat16)
    spread_back = spread_back.reshape(groups, capacity, piece_len, -1)
    returned = lax.all_to_all(spread_back, "bal", split_axis=0, concat_axis=0, tiled=True)
    result = jnp.dot(
        route_onehot.T, returned.reshape(slot_count, -1), preferred_element_type=jnp.float32
    ).astype(jnp.bfloat16)
    return result.reshape(owned_tiles, piece_len, -1)


def solution(mesh):
    return jax.shard_map(
        per_device,
        mesh=mesh,
        in_specs=(
            P("bal", "seq", None),
            P("bal", "seq", None),
            P("seq", None),
            P("seq", None),
            P("bal", None, None, None),
            P("bal"),
            P("bal", None, None),
        ),
        out_specs=P("bal", "seq", None),
        check_vma=False,
    )
```

profile of v0, /device:TPU:32, one launch (start us, length us, event | category | flops | bytes accessed | tf_op | source)
XLA Modules:
  0.0 369.4 jit_solution(7702107884539255839)
XLA Ops:
  6.5 1.8 copy.85
  10.7 11.2 %all-to-all-start = ((bf16[32,1,1]{2,1,0:T(2,128)(2,1)}), bf16[32,1,1]{2,1,0:T(2,128)(2,1)S(1)}, u32[]{:S(2)}, u32[]{:S(2)}) async-start(bf16[32,1,1]{2,1,0:T(2,128)(2,1)} %copy.60), calls=%async_computation | async-start | bytes 32768 | tf_op jit(solution)/shard_map/all_to_all | solution.py:90
  21.9 2.0 copy.86
  23.9 0.9 convolution_convert_fusion
  24.9 3.0 copy.87
  27.9 2.6 all-to-all-done
  30.5 7.2 %all-to-all-start.1 = ((bf16[32,1,8,5120]{3,2,1,0:T(8,128)(2,1)}), bf16[32,1,8,5120]{3,2,1,0:T(8,128)(2,1)S(1)}, u32[]{:S(2)}, u32[]{:S(2)}) async-start(bf16[32,1,8,5120]{3,2,1,0:T(8,128)(2,1)} %bitcast.2), calls=%async_computation.1 | async-start | bytes 5242880 | tf_op jit(solution)/shard_map/all_to_all | solution.py:89
  38.8 76.5 %all-to-all-done.1 = bf16[32,1,8,5120]{3,2,1,0:T(8,128)(2,1)S(1)} async-done(((bf16[32,1,8,5120]{3,2,1,0:T(8,128)(2,1)}), bf16[32,1,8,5120]{3,2,1,0:T(8,128)(2,1)S(1)}, u32[]{:S(2)}, u32[]{:S(2)}) %all-to-all-start.1) | async-done | bytes 2621472 | tf_op jit(solution)/shard_map/all_to_all | solution.py:89
  115.3 1.4 copy.88
  117.3 1.8 copy.89
  120.5 0.9 copy.66
  121.8 0.9 copy.69
  123.1 36.1 %all-gather.5.cloned.1.call-done = bf16[5120,1152]{1,0:T(8,128)(2,1)} async-done(((bf16[160,1152]{1,0:T(8,128)(2,1)}), bf16[5120,1152]{1,0:T(8,128)(2,1)}) %all-gather.5.cloned.1.call-update) | async-done | bytes 11796496 | tf_op jit(solution)/shard_map/all_gather | solution.py:111
  159.2 15.2 %copy.65 = bf16[1152,5120]{1,0:T(8,128)(2,1)} copy(bf16[1152,5120]{0,1:T(8,128)(2,1)} %bitcast.85) | data formatting | bytes 23592960 | tf_op jit(solution)/shard_map/dot_general | solution.py:109
  174.3 47.2 %all-gather.3.cloned.1.call-done = bf16[16,64,5120]{2,1,0:T(8,128)(2,1)} async-done(((bf16[16,8,5120]{2,1,0:T(8,128)(2,1)}), bf16[16,64,5120]{2,1,0:T(8,128)(2,1)}) %all-gather.3.cloned.1.call-update) | async-done | bytes 10485776 | tf_op jit(solution)/shard_map/all_gather | solution.py:103
  221.6 5.6 %convert_reduce_fusion = f32[16,64]{1,0:T(8,128)S(1)} fusion(bf16[16,64,5120]{2,1,0:T(8,128)(2,1)} %all-gather.3.cloned.1.call-done), kind=kLoop, calls=%fused_computation.7 | loop fusion | flops 10484736 | bytes 10489856 | tf_op jit(solution)/shard_map/reduce_sum | solution.py:54
  227.2 1.3 copy-done
  228.5 2.8 fusion.4
  231.4 6.7 %fusion.7 = bf16[16,64,5120]{2,1,0:T(8,128)(2,1)S(1)} fusion(bf16[16,64,5120]{2,1,0:T(8,128)(2,1)S(1)} %copy-done, f32[16,5120]{1,0:T(8,128)S(1)} %get-tuple-element.18, f32[16,5120]{1,0:T(8,128)S(1)} %get-tuple-element.17, f32[16,64]{1,0:T(8,128)S(1)} %add_rsqrt_fusion, f32[16,64]{1,0:T(8,128)S(1)} %broadcast_multiply_fusion), kind=kLoop, calls=%fused_computation.13 | loop fusion | flops 31457280 | bytes 21635072 | tf_op jit(solution)/shard_map/convert_element_type | solution.py:57
  238.1 15.5 %fusion.74 = f32[1024,3,3,128]{0,3,2,1:T(8,128)S(1)} fusion(bf16[1024,5120,1,1]{1,0,3,2:T(8,128)(2,1)S(1)} %bitcast.87, bf16[3,3,128,5120]{3,2,1,0:T(8,128)(2,1)} %bitcast.86), kind=kOutput, calls=%fused_computation.108 | convolution fusion | flops 12079595520 | bytes 27000832 | tf_op jit(solution)/shard_map/dot_general | solution.py:109
  253.7 2.1 copy-done.1
  256.1 13.6 %all-reduce = (f32[1024]{0:T(1024)S(1)}, f32[1024]{0:T(1024)S(1)}) all-reduce(f32[1024]{0:T(1024)S(1)} %get-tuple-element.6, f32[1024]{0:T(1024)S(1)} %get-tuple-element.5), channel_id=1, replica_groups=mesh['bal'=32,'seq'=8] {'seq'}, use_global_device_ids=true, to_apply=%region_14.15 | all-reduce | flops 2048 | bytes 16384 | tf_op jit(solution)/shard_map/psum | solution.py:118
  269.7 2.2 multiply_convert_fusion.1
  272.0 5.1 %fusion.69 = (f32[3,512]{1,0:T(4,128)S(1)}, f32[3,512,1024]{2,1,0:T(8,128)}) fusion(pred[512,1024]{1,0:T(8,128)(4,1)S(1)} %copy.66, bf16[1024,3,128]{0,2,1:T(8,128)(2,1)S(1)} %get-tuple-element.16, bf16[1024,3,128]{0,2,1:T(8,128)(2,1)S(1)} %get-tuple-element.15), kind=kOutput, calls=%fused_computation.107 | convolution fusion | flops 408945664 | bytes 8001536 | tf_op jit(solution)/shard_map/sub | solution.py:66
  277.0 5.1 %fusion.64 = (f32[3,512]{1,0:T(4,128)S(1)}, f32[3,512,1024]{2,1,0:T(8,128)}) fusion(pred[512,1024]{1,0:T(8,128)(4,1)S(1)} %copy.69, bf16[1024,3,128]{0,2,1:T(8,128)(2,1)S(1)} %get-tuple-element.16, bf16[1024,3,128]{0,2,1:T(8,128)(2,1)S(1)} %get-tuple-element.15), kind=kOutput, calls=%fused_computation.106 | convolution fusion | flops 408945664 | bytes 8001536 | tf_op jit(solution)/shard_map/sub | solution.py:66
  282.1 4.7 %fusion.20 = bf16[512,3,128]{0,2,1:T(8,128)(2,1)S(1)} fusion(f32[3,512,1024]{2,1,0:T(8,128)} %get-tuple-element.30, f32[3,512]{1,0:T(4,128)S(1)} %get-tuple-element.29, f32[1024,3,3,128]{0,3,2,1:T(8,128)} %copy-done.1), kind=kOutput, calls=%fused_computation.40 | convolution fusion | flops 405995520 | bytes 7477248 | tf_op jit(solution)/shard_map/hqk,khd->qhd/dot_general | solution.py:69
  287.1 2.7 fusion.21
  289.9 1.0 reshape.312
  290.9 1.4 copy.73
  292.3 15.7 %all_to_all.34 = bf16[16,64,384]{2,0,1:T(8,128)(2,1)S(1)} all-to-all(bf16[16,64,384]{2,0,1:T(8,128)(2,1)S(1)} %copy.73), channel_id=1, replica_groups=mesh['bal'=32,'seq'=8] {'seq'}, dimensions={1} | all-to-all | bytes 1572864 | tf_op jit(solution)/shard_map/all_to_all | solution.py:142
  310.4 49.6 %all_to_all.35 = bf16[32,1,8,3072]{3,2,1,0:T(8,128)(2,1)S(1)} all-to-all(bf16[32,1,8,3072]{3,2,1,0:T(8,128)(2,1)S(1)} %bitcast.93), channel_id=1, replica_groups=mesh['bal'=32,'seq'=8] {'bal'}, dimensions={0} | all-to-all | bytes 3145728 | tf_op jit(solution)/shard_map/all_to_all | solution.py:147
  361.3 1.3 copy.93
  (54 shorter events, 10.5 us)
Async XLA Ops:
  6.5 152.6 %all-gather.5.cloned.1.call-start = ((), (), s32[]{:S(2)}) async-start(), calls=%async_computation.5 | async-start | bytes 12165120 | tf_op jit(solution)/shard_map/all_gather | solution.py:111
  10.7 19.8 %all-to-all-start = ((bf16[32,1,1]{2,1,0:T(2,128)(2,1)}), bf16[32,1,1]{2,1,0:T(2,128)(2,1)S(1)}, u32[]{:S(2)}, u32[]{:S(2)}) async-start(bf16[32,1,1]{2,1,0:T(2,128)(2,1)} %copy.60), calls=%async_computation | async-start | bytes 32768 | tf_op jit(solution)/shard_map/all_to_all | solution.py:90
  30.5 84.8 %all-to-all-start.1 = ((bf16[32,1,8,5120]{3,2,1,0:T(8,128)(2,1)}), bf16[32,1,8,5120]{3,2,1,0:T(8,128)(2,1)S(1)}, u32[]{:S(2)}, u32[]{:S(2)}) async-start(bf16[32,1,8,5120]{3,2,1,0:T(8,128)(2,1)} %bitcast.2), calls=%async_computation.1 | async-start | bytes 5242880 | tf_op jit(solution)/shard_map/all_to_all | solution.py:89
  37.7 183.9 %all-gather.3.cloned.1.call-start = ((), (), s32[]{:S(2)}) async-start(), calls=%async_computation.4 | async-start | bytes 11796480 | tf_op jit(solution)/shard_map/all_gather | solution.py:103
  116.7 2.3 copy-start.5
  116.8 6.0 %copy-start.2 = (f32[1,4,2,5120]{3,2,1,0:T(2,128)S(1)}, f32[1,4,2,5120]{3,2,1,0:T(2,128)}, u32[]{:S(2)}) copy-start(f32[1,4,2,5120]{3,2,1,0:T(2,128)} %param.11) | copy-start | bytes 491524
  221.6 7.0 %copy-start = (bf16[16,64,5120]{2,1,0:T(8,128)(2,1)S(1)}, bf16[16,64,5120]{2,1,0:T(8,128)(2,1)}, u32[]{:S(2)}) copy-start(bf16[16,64,5120]{2,1,0:T(8,128)(2,1)} %all-gather.3.cloned.1.call-done) | copy-start | bytes 31457284
  238.1 31.6 %copy-start.3 = (f32[3,128]{1,0:T(4,128)S(1)}, f32[3,128]{1,0:T(4,128)}, u32[]{:S(2)}) copy-start(f32[3,128]{1,0:T(4,128)} %param.9) | copy-start | bytes 4612
  238.1 31.6 %copy-start.4 = (f32[3,128]{1,0:T(4,128)S(1)}, f32[3,128]{1,0:T(4,128)}, u32[]{:S(2)}) copy-start(f32[3,128]{1,0:T(4,128)} %param.10) | copy-start | bytes 4612
  253.7 2.1 copy-start.1
  282.1 5.0 %copy-start.6 = (f32[3,512,1024]{2,1,0:T(8,128)S(1)}, f32[3,512,1024]{2,1,0:T(8,128)}, u32[]{:S(2)}) copy-start(f32[3,512,1024]{2,1,0:T(8,128)} %get-tuple-element.28) | copy-start | bytes 18874372
Sparse Core Ops, SparseCore 0:
  9.9 149.1 all-gather.4
  161.0 60.5 all-gather.2
where the time goes:
time: 370 us; the launch traced here: 369 us
  waiting for transfers between devices  162 us (44%)
  blocking collectives  78.9 us (21%)
  local copies, waits for them, and re-layouts  38.9 us (11%)
  matrix products  35.4 us (10%)
  other arithmetic  21.5 us (6%)
  starting transfers between devices  18.6 us (5%)
  between operations  13.7 us (4%)
    all_to_all x1, waiting for transfers between devices, per_device(): lax.all_to_all(outbound, 'bal', split_axis=0, concat_axis=0, tiled=True)  76.5 us
    all_to_all x1, blocking collectives, per_device(): lax.all_to_all(spread_back, 'bal', split_axis=0, concat_axis=0, tiled=True)  49.6 us
    all_gather x1, waiting for transfers between devices, per_device(): whole_tiles = lax.all_gather(compact, 'seq', axis=1, tiled=True)  47.2 us
    all_gather x1, waiting for transfers between devices, per_device(): lax.all_gather(flat_weight, 'bal', axis=0, tiled=True)  36.1 us
    unnamed x23, local copies, waits for them, and re-layouts  15.7 us
    all_to_all x1, blocking collectives, per_device(): lax.all_to_all(head_major, 'seq', split_axis=1, concat_axis=2, tiled=True)  15.7 us
    dot_general x1, matrix products, per_device(): jnp.dot(token_rows, lax.all_gather(flat_weight, 'bal', axis=0, tiled=True...  15.5 us
    dot_general x1, local copies, waits for them, and re-layouts, per_device(): jnp.dot(token_rows, lax.all_gather(flat_weight, 'bal', axis=0, tiled=True...  15.2 us
  transfers between devices with their start and end apart: 4, of which 4 were waited for; matrix products, arithmetic and copies ran while one was open for 9% of the time, Pallas kernels for 0%

commit v1 on v0

v1 whole, which is shorter than its diff:
```python
import jax
import jax.numpy as jnp
from jax import lax
from jax.experimental import pallas as pl
from jax.experimental.pallas import tpu as pltpu
from jax.sharding import PartitionSpec as P

HEADS = 24
HD = 128
TILES_OWN = 16
NX, NZ, NY = 4, 8, 4
N_BAL = NX * NZ
N_SEQ = 2 * NY
ROWS_B = 128

eps_norm = 1e-06
score_fill = -1e30
MESH = pl.DeviceIdType.MESH


def tile_layout(clip_shape):
    frames_of = clip_shape[:, 0]
    rows_of = clip_shape[:, 1]
    cols_of = clip_shape[:, 2]
    clip_sizes = frames_of * rows_of * cols_of
    clips = jnp.arange(clip_shape.shape[0], dtype=jnp.int32)
    upto = clips[None, :] <= clips[:, None]
    clip_ends = jnp.sum(jnp.where(upto, clip_sizes[None, :], 0), axis=1)
    clip_starts = clip_ends - clip_sizes
    local_index = jnp.arange(TILES_OWN, dtype=jnp.int32)
    member = jnp.sum((local_index[:, None] >= clip_ends[None, :]).astype(jnp.int32), axis=1)
    onehot = member[:, None] == clips[None, :]

    def select_clip(values):
        return jnp.sum(jnp.where(onehot, values[None, :], 0), axis=1)

    offset = local_index - select_clip(clip_starts)
    height = jnp.maximum(select_clip(rows_of), 1)
    width_tiles = jnp.maximum(select_clip(cols_of), 1)
    frame_index = offset // (height * width_tiles)
    row_index = offset // width_tiles % height
    column = offset % width_tiles

    def within_one(coords):
        return jnp.abs(coords[:, None] - coords[None, :]) <= 1

    tile_mask = (
        (member[:, None] == member[None, :])
        & within_one(frame_index)
        & within_one(row_index)
        & within_one(column)
    )
    return (member, tile_mask)


def attend(q_block, key_rows, values, block_mask):
    scores = jnp.einsum(
        "qhd,khd->hqk", q_block, key_rows, preferred_element_type=jnp.float32
    ) * key_rows.shape[2] ** (-0.5)
    scores = jnp.where(block_mask[None], scores, score_fill)
    largest = jnp.max(scores, axis=-1, keepdims=True)
    exp_scores = jnp.exp(scores - largest)
    totals = jnp.sum(exp_scores, axis=-1, keepdims=True)
    weights = (exp_scores / totals).astype(jnp.bfloat16)
    return jnp.einsum("hqk,khd->qhd", weights, values, preferred_element_type=jnp.float32)


def project_kernel(
    slot_tile, source_of, clip_of, tok, w_in, mod, out,
    wbuf, gbuf, obuf, rbuf,
    rel_s, rel_r, z_s, z_r, x_s, x_r, xf_s, xf_r, ax_s, ax_r, axf_s, axf_r, az_s, az_r,
    y_s, y_r, yf_s, yf_r, c_s, c_r,
):
    me = lax.axis_index("bal")
    sq = lax.axis_index("seq")
    x, z = me // NZ, me % NZ
    y, core = sq // 2, sq % 2
    d_model = tok.shape[2]
    k_group = d_model // NX
    rows = w_in.shape[1]
    half_b = ROWS_B // 2
    half_a = (rows - ROWS_B) // 2

    def bal(bx, bz):
        return {"bal": (bx % NX) * NZ + bz % NZ}

    def seq(sy, sc):
        return {"seq": (sy % NY) * 2 + sc}

    z_up, z_dn = bal(x, z + 1), bal(x, z + NZ - 1)
    x_up, x_dn = bal(x + 1, z), bal(x + NX - 1, z)
    y_up, y_dn = seq(y + 1, core), seq(y + NY - 1, core)
    other = seq(y, 1 - core)

    def copy(ref, send, recv, where):
        return pltpu.make_async_remote_copy(
            src_ref=ref, dst_ref=ref, send_sem=send, recv_sem=recv,
            device_id=where, device_id_type=MESH,
        )

    started = []

    def go(ref, send, recv, where):
        c = copy(ref, send, recv, where)
        c.start()
        started.append(c)

    def arrived(ref, send, recv):
        copy(ref, send, recv, z_up).wait_recv()

    barrier = pltpu.get_barrier_semaphore()

    @pl.loop(1, N_BAL)
    def _(d):
        pl.semaphore_signal(barrier, inc=1, device_id={"bal": (me + d) % N_BAL}, device_id_type=MESH)

    @pl.loop(1, N_SEQ)
    def _(d):
        pl.semaphore_signal(barrier, inc=1, device_id={"seq": (sq + d) % N_SEQ}, device_id_type=MESH)

    for h in range(w_in.shape[0]):
        wbuf[x, z, :, h * 384 : (h + 1) * 384] = w_in[h]
    pl.semaphore_wait(barrier, N_BAL + N_SEQ - 2)

    def b_piece(bx, bz, lo=0, size=ROWS_B):
        return wbuf.at[bx % NX, bz % NZ, pl.ds(lo, size)]

    def a_piece(bx, bz, lo=0, size=rows - ROWS_B):
        return wbuf.at[bx % NX, bz % NZ, pl.ds(ROWS_B + lo, size)]

    def a_block(bz, lo=0, size=NX):
        return wbuf.at[pl.ds(lo, size), bz % NZ, pl.ds(ROWS_B, rows - ROWS_B)]

    go(b_piece(x, z), z_s.at[0, 1], z_r.at[0, 1], z_up)
    go(b_piece(x, z), z_s.at[1, 1], z_r.at[1, 1], z_dn)
    go(a_piece(x, z), ax_s.at[0], ax_r.at[0], x_up)
    go(a_piece(x, z), ax_s.at[1], ax_r.at[1], x_dn)

    rbuf[me] = tok[slot_tile[me]]

    def relay(d):
        to = (me + d) % N_BAL
        return pltpu.make_async_remote_copy(
            src_ref=obuf.at[to], dst_ref=rbuf.at[me], send_sem=rel_s.at[d], recv_sem=rel_r.at[d],
            device_id={"bal": to}, device_id_type=MESH,
        )

    @pl.loop(1, N_BAL)
    def _(d):
        to = (me + d) % N_BAL
        obuf[to] = tok[slot_tile[to]]
        relay(d).start()

    def send_x(j, bz):
        go(b_piece(x, bz), x_s.at[0, j], x_r.at[0, j], x_up)
        go(b_piece(x, bz), x_s.at[1, j], x_r.at[1, j], x_dn)

    def pass_x(j, bz):
        arrived(b_piece(x + NX - 1, bz), x_s.at[0, j], x_r.at[0, j])
        go(b_piece(x + NX - 1, bz, 0, half_b), xf_s.at[0, j], xf_r.at[0, j], x_up)
        arrived(b_piece(x + 1, bz), x_s.at[1, j], x_r.at[1, j])
        go(b_piece(x + 1, bz, half_b, half_b), xf_s.at[1, j], xf_r.at[1, j], x_dn)

    send_x(0, z)
    arrived(a_piece(x + NX - 1, z), ax_s.at[0], ax_r.at[0])
    go(a_piece(x + NX - 1, z, 0, half_a), axf_s.at[0], axf_r.at[0], x_up)
    arrived(a_piece(x + 1, z), ax_s.at[1], ax_r.at[1])
    go(a_piece(x + 1, z, half_a, half_a), axf_s.at[1], axf_r.at[1], x_dn)

    def step_z(k):
        if k < NZ // 2:
            size, lo = (ROWS_B, 0) if k < NZ // 2 - 1 else (half_b, half_b)
            arrived(b_piece(x, z + NZ - k), z_s.at[0, k], z_r.at[0, k])
            go(b_piece(x, z + NZ - k, 0, size), z_s.at[0, k + 1], z_r.at[0, k + 1], z_up)
            arrived(b_piece(x, z + k), z_s.at[1, k], z_r.at[1, k])
            go(b_piece(x, z + k, lo, size), z_s.at[1, k + 1], z_r.at[1, k + 1], z_dn)
            send_x(NZ - k, z + NZ - k)
            send_x(k, z + k)
        else:
            arrived(b_piece(x, z + k, 0, half_b), z_s.at[0, k], z_r.at[0, k])
            arrived(b_piece(x, z + k, half_b, half_b), z_s.at[1, k], z_r.at[1, k])
            send_x(k, z + k)

    def step_az(k):
        if k < NZ // 2:
            size, lo = (NX, 0) if k < NZ // 2 - 1 else (NX // 2, NX // 2)
            arrived(a_block(z + NZ - k), az_s.at[0, k], az_r.at[0, k])
            go(a_block(z + NZ - k, 0, size), az_s.at[0, k + 1], az_r.at[0, k + 1], z_up)
            arrived(a_block(z + k), az_s.at[1, k], az_r.at[1, k])
            go(a_block(z + k, lo, size), az_s.at[1, k + 1], az_r.at[1, k + 1], z_dn)
        else:
            arrived(a_block(z + k, 0, NX // 2), az_s.at[0, k], az_r.at[0, k])
            arrived(a_block(z + k, NX // 2, NX // 2), az_s.at[1, k], az_r.at[1, k])

    step_z(1)
    arrived(a_piece(x + 2, z, 0, half_a), axf_s.at[0], axf_r.at[0])
    arrived(a_piece(x + 2, z, half_a, half_a), axf_s.at[1], axf_r.at[1])
    go(a_block(z), az_s.at[0, 1], az_r.at[0, 1], z_up)
    go(a_block(z), az_s.at[1, 1], az_r.at[1, 1], z_dn)
    pass_x(0, z)
    step_z(2)
    step_z(3)
    step_az(1)
    pass_x(1, z + 1)
    pass_x(NZ - 1, z + NZ - 1)
    step_z(4)
    step_az(2)

    @pl.loop(1, N_BAL)
    def _(d):
        came = (me + N_BAL - d) % N_BAL
        pltpu.make_async_remote_copy(
            src_ref=obuf.at[me], dst_ref=rbuf.at[came], send_sem=rel_s.at[d], recv_sem=rel_r.at[d],
            device_id={"bal": came}, device_id_type=MESH,
        ).wait_recv()

    tokens_per = tok.shape[1]

    @pl.loop(0, TILES_OWN)
    def _(r):
        values = rbuf[source_of[r]].astype(jnp.float32)
        center = jnp.mean(values, axis=-1, keepdims=True)
        away = values - center
        spread = jnp.mean(away * away, axis=-1, keepdims=True)
        clip = clip_of[r]
        shift = mod[clip, 0:1, :]
        scale = mod[clip, 1:2, :]
        normed = away * lax.rsqrt(spread + eps_norm) * (1.0 + scale) + shift
        gbuf[sq, r] = normed.astype(jnp.bfloat16)

    half_t = TILES_OWN // 2

    def piece(sy, sc, lo=0, size=TILES_OWN):
        return gbuf.at[(sy % NY) * 2 + sc, pl.ds(lo, size)]

    go(piece(y, core), y_s.at[0], y_r.at[0], y_up)
    go(piece(y, core), y_s.at[1], y_r.at[1], y_dn)
    go(piece(y, core), c_s.at[0], c_r.at[0], other)

    step_az(3)
    pass_x(2, z + 2)
    pass_x(NZ - 2, z + NZ - 2)
    step_az(4)
    pass_x(3, z + 3)
    pass_x(NZ - 3, z + NZ - 3)

    arrived(piece(y + NY - 1, core), y_s.at[0], y_r.at[0])
    go(piece(y + NY - 1, core, 0, half_t), yf_s.at[0], yf_r.at[0], y_up)
    go(piece(y + NY - 1, core), c_s.at[1], c_r.at[1], other)
    arrived(piece(y + 1, core), y_s.at[1], y_r.at[1])
    go(piece(y + 1, core, half_t, half_t), yf_s.at[1], yf_r.at[1], y_dn)
    go(piece(y + 1, core), c_s.at[2], c_r.at[2], other)
    pass_x(4, z + 4)

    for j in range(NZ):
        arrived(b_piece(x + 2, z + j, 0, half_b), xf_s.at[0, j], xf_r.at[0, j])
        arrived(b_piece(x + 2, z + j, half_b, half_b), xf_s.at[1, j], xf_r.at[1, j])

    arrived(piece(y + 2, core, 0, half_t), yf_s.at[0], yf_r.at[0])
    go(piece(y + 2, core, 0, half_t), c_s.at[3], c_r.at[3], other)
    arrived(piece(y + 2, core, half_t, half_t), yf_s.at[1], yf_r.at[1])
    go(piece(y + 2, core, half_t, half_t), c_s.at[4], c_r.at[4], other)
    arrived(piece(y, 1 - core), c_s.at[0], c_r.at[0])
    arrived(piece(y + NY - 1, 1 - core), c_s.at[1], c_r.at[1])
    arrived(piece(y + 1, 1 - core), c_s.at[2], c_r.at[2])
    arrived(piece(y + 2, 1 - core, 0, half_t), c_s.at[3], c_r.at[3])
    arrived(piece(y + 2, 1 - core, half_t, half_t), c_s.at[4], c_r.at[4])

    m = N_SEQ * TILES_OWN * tokens_per
    for g in range(NX):
        @pl.loop(0, 3)
        def _(n):
            cols = pl.ds(pl.multiple_of(n * 384, 128), 384)
            left = gbuf[:, :, :, g * k_group : (g + 1) * k_group].reshape(m, k_group)
            right = wbuf[g, :, :, cols].reshape(k_group, 384)
            part = jnp.dot(left, right, preferred_element_type=jnp.float32)
            if g == 0:
                out[:, cols] = part
            else:
                out[:, cols] += part

    @pl.loop(1, N_BAL)
    def _(d):
        relay(d).wait_send()

    for c in started:
        c.wait_send()


def project(slot_tile, source_of, clip_of, tokens, w_heads, mod_table):
    tiles, per, d_model = tokens.shape
    heads, rows, width = w_heads.shape
    dma = pltpu.SemaphoreType.DMA
    vmem = pl.BlockSpec(memory_space=pltpu.VMEM)
    smem = pl.BlockSpec(memory_space=pltpu.SMEM)
    m = N_SEQ * tiles * per
    return pl.pallas_call(
        project_kernel,
        out_shape=jax.ShapeDtypeStruct((m, heads * width), jnp.float32),
        in_specs=[smem] * 3 + [vmem] * 3,
        out_specs=vmem,
        scratch_shapes=[
            pltpu.VMEM((NX, NZ, rows, heads * width), jnp.bfloat16),
            pltpu.VMEM((N_SEQ, tiles, per, d_model), jnp.bfloat16),
            pltpu.VMEM((N_BAL, per, d_model), jnp.bfloat16),
            pltpu.VMEM((N_BAL, per, d_model), jnp.bfloat16),
            dma((N_BAL,)), dma((N_BAL,)),
            dma((2, 5)), dma((2, 5)),
            dma((2, NZ)), dma((2, NZ)),
            dma((2, NZ)), dma((2, NZ)),
            dma((2,)), dma((2,)), dma((2,)), dma((2,)),
            dma((2, 5)), dma((2, 5)),
            dma((2,)), dma((2,)), dma((2,)), dma((2,)),
            dma((5,)), dma((5,)),
        ],
        compiler_params=pltpu.CompilerParams(
            collective_id=0, has_side_effects=True, vmem_limit_bytes=58 * 2**20
        ),
        cost_estimate=pl.CostEstimate(
            flops=2 * m * d_model * heads * width, bytes_accessed=8 * 2**20, transcendentals=0
        ),
        name="relay_norm_project",
    )(slot_tile, source_of, clip_of, tokens, w_heads, mod_table)


def per_device(tokens, w_qkv, q_gain, k_gain, modulation, tile_owner, clip_dims):
    me = lax.axis_index("bal")
    owned_tiles, piece_len, width_model = tokens.shape
    owners = jnp.arange(N_BAL, dtype=jnp.int32)
    tile_ids = jnp.arange(owned_tiles, dtype=jnp.int32)
    slot_tile = jnp.sum(
        jnp.where(tile_owner[None, :] == owners[:, None], tile_ids[None, :], 0), axis=1
    )
    every_owner = lax.all_gather(tile_owner, "bal", axis=0, tiled=True).reshape(N_BAL, owned_tiles)
    gives = jnp.sum((every_owner == me).astype(jnp.int32), axis=1)
    position = jnp.sum(jnp.where(owners[None, :] < owners[:, None], gives[None, :], 0), axis=1)
    source_of = jnp.sum(
        jnp.where((position[None, :] == tile_ids[:, None]) & (gives[None, :] > 0), owners[None, :], 0),
        axis=1,
    )
    member, tile_mask = tile_layout(clip_dims[0])
    projected = project(
        slot_tile, source_of, member, tokens, w_qkv.transpose(1, 0, 2), modulation[0]
    )
    per_dev_heads = q_gain.shape[0]
    total_tokens = projected.shape[0]
    projected = projected.reshape(total_tokens, per_dev_heads, 3, -1)
    query = projected[:, :, 0]
    keyed = projected[:, :, 1]
    valued = projected[:, :, 2].astype(jnp.bfloat16)
    sums_q, sums_k = lax.psum(
        (jnp.sum(jnp.square(query), axis=(1, 2)), jnp.sum(jnp.square(keyed), axis=(1, 2))), "seq"
    )
    features = HEADS * query.shape[2]
    q_normed = (
        query * lax.rsqrt(sums_q / features + eps_norm)[:, None, None] * q_gain[None]
    ).astype(jnp.bfloat16)
    k_normed = (
        keyed * lax.rsqrt(sums_k / features + eps_norm)[:, None, None] * k_gain[None]
    ).astype(jnp.bfloat16)
    token_mask = jnp.tile(
        jnp.repeat(jnp.repeat(tile_mask, piece_len, axis=0), piece_len, axis=1), (N_SEQ, N_SEQ)
    )
    block_rows = min(512, total_tokens)
    outputs = []
    for block_start in range(0, total_tokens, block_rows):
        outputs.append(
            attend(
                q_normed[block_start : block_start + block_rows],
                k_normed,
                valued,
                token_mask[block_start : block_start + block_rows],
            )
        )
    attended = jnp.concatenate(outputs, axis=0).astype(jnp.bfloat16)
    by_token_group = attended.reshape(N_SEQ, TILES_OWN * piece_len, -1)
    per_token = lax.all_to_all(by_token_group, "seq", split_axis=0, concat_axis=2, tiled=True)
    collect = (source_of[:, None] == owners[None, :]).astype(jnp.bfloat16)
    spread_back = jnp.dot(
        collect.T, per_token.reshape(TILES_OWN, -1), preferred_element_type=jnp.float32
    ).astype(jnp.bfloat16)
    spread_back = spread_back.reshape(N_BAL, 1, piece_len, -1)
    returned = lax.all_to_all(spread_back, "bal", split_axis=0, concat_axis=0, tiled=True)
    route = (tile_owner[:, None] == owners[None, :]).astype(jnp.bfloat16)
    result = jnp.dot(
        route, returned.reshape(N_BAL, -1), preferred_element_type=jnp.float32
    ).astype(jnp.bfloat16)
    return result.reshape(owned_tiles, piece_len, -1)


def solution(mesh):
    return jax.shard_map(
        per_device,
        mesh=mesh,
        in_specs=(
            P("bal", "seq", None),
            P("bal", "seq", None),
            P("seq", None),
            P("seq", None),
            P("bal", None, None, None),
            P("bal"),
            P("bal", None, None),
        ),
        out_specs=P("bal", "seq", None),
        check_vma=False,
    )
```

time: 370 us -> 317 us (0.86)
  Pallas kernels: 0 us -> 172 us
  waiting for transfers between devices: 162 us -> 0 us
  local copies, waits for them, and re-layouts: 38.9 us -> 17.7 us
  blocking collectives: 78.9 us -> 98.9 us
  starting transfers between devices: 18.6 us -> 0 us
  other arithmetic: 21.5 us -> 5.37 us
  matrix products: 35.4 us -> 21.7 us
  between operations: 13.7 us -> 0.96 us
    pallas_call x0 -> x1, Pallas kernels: none -> 172 us  [project(): pl.pallas_call(project_kernel, out_shape=jax.ShapeDtypeStruct((m, heads *...]
    all_gather x2 -> x0, waiting for transfers between devices: 83.3 us -> none  [the longest x1 47.2 us: per_device(): whole_tiles = lax.all_gather(compact, 'seq', axis=1, tiled=True)]
    all_to_all x2 -> x0, waiting for transfers between devices: 79.1 us -> none  [the longest x1 76.5 us: per_device(): lax.all_to_all(outbound, 'bal', split_axis=0, concat_axis=0, tiled=True)]
    unnamed x0 -> x1, blocking collectives: none -> 22.6 us
    all_to_all x2 -> x0, starting transfers between devices: 18.4 us -> none  [the longest x1 11.2 us: per_device(): lax.all_to_all(filled, 'bal', split_axis=0, concat_axis=0, tiled=True)]
    dot_general x4 -> x1, matrix products: 17.4 us -> 0.42 us  [per_device(): jnp.dot(route, returned.reshape(N_BAL, -1), preferred_element_type=jnp.fl...]
    dot_general x1 -> x0, local copies, waits for them, and re-layouts: 15.2 us -> none  [per_device(): jnp.dot(token_rows, lax.all_gather(flat_weight, 'bal', axis=0, tiled=True...]
    unnamed x23 -> x24, local copies, waits for them, and re-layouts: 15.7 us -> 8.11 us
  transfers between devices with their start and end apart: 4 -> 0, of which waited for: 4 -> 0; matrix products, arithmetic and copies ran while one was open for 9% -> 0% of each run, Pallas kernels for 0% -> 0%
where the time goes in v1:
time: 317 us
  Pallas kernels  172 us (54%)
  blocking collectives  98.9 us (31%)
  matrix products  21.7 us (7%)
  local copies, waits for them, and re-layouts  17.7 us (6%)
  other arithmetic  5.37 us (2%)
    pallas_call x1, Pallas kernels, project(): pl.pallas_call(project_kernel, out_shape=jax.ShapeDtypeStruct((m, heads *...  172 us
    all_to_all x1, blocking collectives, per_device(): lax.all_to_all(spread_back, 'bal', split_axis=0, concat_axis=0, tiled=True)  44.1 us
    unnamed x1, blocking collectives  22.6 us
    psum x1, blocking collectives, per_device(): lax.psum((jnp.sum(jnp.square(query), axis=(1, 2)), jnp.sum(jnp.square(key...  16.5 us
    all_to_all x1, blocking collectives, per_device(): lax.all_to_all(by_token_group, 'seq', split_axis=0, concat_axis=2, tiled=...  15.7 us
    sub x2, matrix products, attend(): exp_scores = jnp.exp(scores - largest)  13.3 us
    unnamed x24, local copies, waits for them, and re-layouts  8.11 us
    dot_general x2, matrix products, attend(): jnp.einsum('hqk,khd->qhd', weights, values, preferred_element_type=jnp.fl...  7.32 us

profile of v1, /device:TPU:32, one launch (start us, length us, event | category | flops | bytes accessed | tf_op | source)
XLA Modules:
  0.0 316.6 jit_solution(4508192530950001545)
XLA Ops:
  0.0 0.8 copy.40
  1.1 0.6 convert_reduce_fusion.clip_of
  1.7 1.2 select_reduce_fusion.1.slot_tile
  2.9 1.3 dynamic-slice
  5.0 0.9 dynamic-update-slice
  5.8 22.6 %all-reduce = s32[512]{0:T(512)S(1)} all-reduce(s32[512]{0:T(512)S(1)} %dynamic-update-slice), channel_id=1, replica_groups=mesh['bal'=32,'seq'=8] {'bal'}, use_global_device_ids=true, to_apply=%add | all-reduce | flops 512 | bytes 4096
  28.8 0.6 select_reduce_fusion.2.source_of
  29.4 171.9 %relay_norm_project.1 = f32[1024,1152]{1,0:T(8,128)} custom-call(s32[32]{0:T(128)} %select_reduce_fusion.1.slot_tile, s32[16]{0:T(128)} %select_reduce_fusion.2.source_of, s32[16]{0:T(128)} %convert_reduce_fusion.clip_of, bf16[16,8,5120]{2,1,0:T(8,128)(2,1)} %tok.1, bf16[3,160,384]{2,1,0:T(8,128)(2,1)} %bitcast.84, f32[4,2,5120]{2,1,0:T(2,128)} %bitcast.85), custom_call_target="tpu_custom_call" | custom-call | flops 12079595520 | bytes 8388608 | tf_op jit(solution)/shard_map/relay_norm_project/pallas_call | solution.py:297
  201.4 6.1 %copy.41 = f32[1024,1152]{0,1:T(8,128)} copy(f32[1024,1152]{1,0:T(8,128)} %relay_norm_project.1) | data formatting | bytes 9437184 | tf_op jit(solution)/shard_map/relay_norm_project/pallas_call | solution.py:297
  207.4 1.6 multiply_reduce_fusion
  209.0 1.5 slice.41
  210.6 0.3 and_select_fusion.3
  211.4 1.0 copy.66
  212.4 0.5 copy.53
  212.9 0.2 fusion.12
  213.1 16.5 %all-reduce.1 = (f32[1024]{0:T(1024)S(1)}, f32[1024]{0:T(1024)S(1)}) all-reduce(f32[1024]{0:T(1024)S(1)} %multiply_reduce_fusion, f32[1024]{0:T(1024)S(1)} %fusion.12), channel_id=1, replica_groups=mesh['bal'=32,'seq'=8] {'seq'}, use_global_device_ids=true, to_apply=%region_12.13 | all-reduce | flops 2048 | bytes 16384 | tf_op jit(solution)/shard_map/psum | solution.py:351
  229.6 0.2 fusion.14
  229.9 6.7 %fusion.55 = (f32[3,512]{1,0:T(4,128)S(1)}, f32[3,512,1024]{2,1,0:T(8,128)}) fusion(pred[512,1024]{1,0:T(8,128)(4,1)} %bitcast.81, bf16[1024,3,128]{2,0,1:T(8,128)(2,1)S(1)} %fusion.14, f32[1024,3,3,128]{0,3,2,1:T(8,128)} %bitcast.68, f32[3,128]{1,0:T(4,128)S(1)} %copy-done.5, f32[1024]{0:T(1024)S(1)} %get-tuple-element.20), kind=kOutput, calls=%fused_computation.92 | convolution fusion | flops 410125312 | bytes 8794112 | tf_op jit(solution)/shard_map/sub | solution.py:62
  236.6 6.6 %fusion.50 = (f32[3,512]{1,0:T(4,128)S(1)}, f32[3,512,1024]{2,1,0:T(8,128)}) fusion(pred[512,1024]{1,0:T(8,128)(4,1)S(1)} %bitcast.82, bf16[1024,3,128]{2,0,1:T(8,128)(2,1)S(1)} %fusion.14, f32[1024,3,3,128]{0,3,2,1:T(8,128)} %bitcast.69, f32[3,128]{1,0:T(4,128)S(1)} %copy-done.5, f32[1024]{0:T(1024)S(1)} %get-tuple-element.20), kind=kOutput, calls=%fused_computation.91 | convolution fusion | flops 410125312 | bytes 8794112 | tf_op jit(solution)/shard_map/sub | solution.py:62
  243.2 4.7 %fusion.17 = bf16[512,3,128]{0,2,1:T(8,128)(2,1)S(1)} fusion(f32[3,512,1024]{2,1,0:T(8,128)} %get-tuple-element.19, f32[3,512]{1,0:T(4,128)S(1)} %get-tuple-element.18, f32[1024,3,3,128]{0,3,2,1:T(8,128)} %bitcast.70), kind=kOutput, calls=%fused_computation.32 | convolution fusion | flops 405995520 | bytes 7477248 | tf_op jit(solution)/shard_map/hqk,khd->qhd/dot_general | solution.py:65
  247.9 0.4 copy-done.6
  248.3 2.7 fusion.18
  251.2 0.6 copy.48
  251.8 15.7 %all_to_all.20 = bf16[8,128,384]{2,1,0:T(8,128)(2,1)S(1)} all-to-all(bf16[8,128,384]{2,1,0:T(8,128)(2,1)S(1)} %copy.48), channel_id=1, replica_groups=mesh['bal'=32,'seq'=8] {'seq'}, dimensions={0} | all-to-all | bytes 1572864 | tf_op jit(solution)/shard_map/all_to_all | solution.py:377
  267.5 0.5 copy.49
  267.9 0.4 reshape.205
  268.3 0.7 convolution_convert_fusion
  269.0 0.9 copy.57
  269.9 44.1 %all_to_all.21 = bf16[32,1,8,3072]{3,2,1,0:T(8,128)(2,1)S(1)} all-to-all(bf16[32,1,8,3072]{3,2,1,0:T(8,128)(2,1)S(1)} %bitcast.73), channel_id=1, replica_groups=mesh['bal'=32,'seq'=8] {'bal'}, dimensions={0} | all-to-all | bytes 3145728 | tf_op jit(solution)/shard_map/all_to_all | solution.py:383
  314.0 0.9 copy.58
  314.8 0.4 convolution_convert_fusion.1
  315.3 1.3 copy.59
  (33 shorter events, 1.5 us)
Async XLA Ops:
  207.4 3.1 copy-start.1
  209.0 20.6 %copy-start.2 = (f32[3,128]{1,0:T(4,128)S(1)}, f32[3,128]{1,0:T(4,128)}, u32[]{:S(2)}) copy-start(f32[3,128]{1,0:T(4,128)} %param.9) | copy-start | bytes 4612
  210.5 19.4 %copy-start.5 = (f32[3,128]{1,0:T(4,128)S(1)}, f32[3,128]{1,0:T(4,128)}, u32[]{:S(2)}) copy-start(f32[3,128]{1,0:T(4,128)} %param.10) | copy-start | bytes 4612
  229.9 6.7 %copy-start = (pred[64,8,8,128]{3,1,2,0:T(8,128)(4,1)S(1)}, pred[64,8,8,128]{3,1,2,0:T(8,128)(4,1)}, u32[]{:S(2)}) copy-start(pred[64,8,8,128]{3,1,2,0:T(8,128)(4,1)} %copy.66) | copy-start | bytes 1572868
  243.2 5.0 %copy-start.6 = (f32[3,512,1024]{2,1,0:T(8,128)S(1)}, f32[3,512,1024]{2,1,0:T(8,128)}, u32[]{:S(2)}) copy-start(f32[3,512,1024]{2,1,0:T(8,128)} %get-tuple-element.17) | copy-start | bytes 18874372
  250.9 17.4 %copy-start.4 = (s32[16]{0:T(128)S(1)}, s32[16]{0:T(128)}, u32[]{:S(2)}) copy-start(s32[16]{0:T(128)} %select_reduce_fusion.2.source_of) | copy-start | bytes 196
  269.0 45.9 %copy-start.3 = (s32[16]{0:T(128)S(1)}, s32[16]{0:T(128)}, u32[]{:S(2)}) copy-start(s32[16]{0:T(128)} %param.12) | copy-start | bytes 196

commit v2 on v1

v2 whole, which is shorter than its diff:
```python
import jax
import jax.numpy as jnp
from jax import lax
from jax.experimental import pallas as pl
from jax.experimental.pallas import tpu as pltpu
from jax.sharding import PartitionSpec as P

HEADS = 24
HD = 128
TILES_OWN = 16
NX, NZ, NY = 4, 8, 4
N_BAL = NX * NZ
N_SEQ = 2 * NY
MAXCLIPS = 4
PER = 8
GROUP = TILES_OWN * PER
LOCAL_HEADS = HEADS // N_SEQ
WIDTH = 3 * HD
ROWS_B = 128
ORDER = ("R0", "X0", "AF", "Z1", "A0", "P0", "P1", "R", "Z2", "A1", "Z3", "P2", "A2", "Z4", "P3", "A3", "Y1", "P4", "A4", "F", "Y2")

eps_norm = 1e-06
score_fill = -1e30
LOG2_E = 1.4426950408889634
MESH = pl.DeviceIdType.MESH


def kernel(
    tile_owner, clip_dims, tok, w_in, mod, q_gain, k_gain, out,
    wbuf, gbuf, obuf, rbuf, acc, row_own, row_all, place, sums, bias, qn, kn, vn, att, heads, back, came_back, place_s,
    rel_s, rel_r, z_s, z_r, x_s, x_r, xf_s, xf_r, ax_s, ax_r, axf_s, axf_r, az_s, az_r,
    y_s, y_r, yf_s, yf_r, c_s, c_r, own_s, own_r, place_sem, sum_s, sum_r, att_s, att_r, ret_s, ret_r,
):
    me = lax.axis_index("bal")
    sq = lax.axis_index("seq")
    x, z = me // NZ, me % NZ
    y, core = sq // 2, sq % 2
    d_model = tok.shape[2]
    k_group = d_model // NX
    rows = w_in.shape[1]
    half_b = ROWS_B // 2
    half_a = (rows - ROWS_B) // 2
    half_t = TILES_OWN // 2

    def bal(bx, bz):
        return {"bal": (bx % NX) * NZ + bz % NZ}

    def seq(sy, sc):
        return {"seq": (sy % NY) * 2 + sc}

    z_up, z_dn = bal(x, z + 1), bal(x, z + NZ - 1)
    x_up, x_dn = bal(x + 1, z), bal(x + NX - 1, z)
    y_up, y_dn = seq(y + 1, core), seq(y + NY - 1, core)
    other = seq(y, 1 - core)

    def move(src, dst, send, recv, where):
        return pltpu.make_async_remote_copy(
            src_ref=src, dst_ref=dst, send_sem=send, recv_sem=recv, device_id=where, device_id_type=MESH
        )

    started = []

    def go(ref, send, recv, where):
        c = move(ref, ref, send, recv, where)
        c.start()
        started.append(c)

    def arrived(ref, send, recv):
        move(ref, ref, send, recv, z_up).wait_recv()

    barrier = pltpu.get_barrier_semaphore()

    @pl.loop(1, N_BAL)
    def _(d):
        pl.semaphore_signal(barrier, inc=1, device_id={"bal": (me + d) % N_BAL}, device_id_type=MESH)

    @pl.loop(1, N_SEQ)
    def _(d):
        pl.semaphore_signal(barrier, inc=1, device_id={"seq": (sq + d) % N_SEQ}, device_id_type=MESH)

    for h in range(LOCAL_HEADS):
        wbuf[x, z, :, h * WIDTH : (h + 1) * WIDTH] = w_in[h]
    lane8 = lax.broadcasted_iota(jnp.int32, (8, 128), 1)
    owners_row = jnp.full((8, 128), -1, jnp.int32)
    for i in range(TILES_OWN):
        owners_row = jnp.where(lane8 == i, tile_owner[i], owners_row)
    row_own[...] = owners_row
    row_all[me] = owners_row

    ends, sizes = [], []
    total = 0
    for k in range(MAXCLIPS):
        f, h, w = (clip_dims[3 * k + i] for i in range(3))
        total = total + f * h * w
        ends.append(total)
        sizes.append((h, w))

    def clip_at(index):
        return sum((index >= ends[k]).astype(jnp.int32) for k in range(MAXCLIPS))

    def layout(index):
        member = clip_at(index)
        start, height, width = (jnp.zeros_like(index) for _ in range(3))
        for k in range(MAXCLIPS):
            here = member == k
            start = jnp.where(here, ends[k - 1] if k else 0, start)
            height = jnp.where(here, sizes[k][0], height)
            width = jnp.where(here, sizes[k][1], width)
        offset = index - start
        frame = (offset >= height * width).astype(jnp.int32)
        offset = offset - frame * height * width
        row = (offset >= width).astype(jnp.int32) + (offset >= 2 * width).astype(jnp.int32)
        return member, frame, row, offset - row * width

    of_query = layout(lax.broadcasted_iota(jnp.int32, (GROUP, GROUP), 0) // PER)
    of_key = layout(lax.broadcasted_iota(jnp.int32, (GROUP, GROUP), 1) // PER)
    allowed = of_query[0] == of_key[0]
    for a, b in zip(of_query[1:], of_key[1:], strict=True):
        allowed = allowed & (jnp.abs(a - b) <= 1)
    bias_tile = jnp.where(allowed, 0.0, score_fill)
    for s in range(N_SEQ):
        bias[:, s * GROUP : (s + 1) * GROUP] = bias_tile

    pl.semaphore_wait(barrier, N_BAL + N_SEQ - 2)

    def b_piece(bx, bz, lo=0, size=ROWS_B):
        return wbuf.at[bx % NX, bz % NZ, pl.ds(lo, size)]

    def a_piece(bx, bz, lo=0, size=rows - ROWS_B):
        return wbuf.at[bx % NX, bz % NZ, pl.ds(ROWS_B + lo, size)]

    def a_block(bz, lo=0, size=NX):
        return wbuf.at[pl.ds(lo, size), bz % NZ, pl.ds(ROWS_B, rows - ROWS_B)]

    def owner_row(d, to, slot):
        return move(row_own, row_all.at[slot], own_s.at[d], own_r.at[d], {"bal": to})

    def relay(d, to, slot):
        return move(obuf.at[to], rbuf.at[slot], rel_s.at[d], rel_r.at[d], {"bal": to})

    def back_relay(d, to, slot):
        return move(back.at[to], came_back.at[slot], ret_s.at[d], ret_r.at[d], {"bal": to})

    def send_x(j, bz):
        go(b_piece(x, bz), x_s.at[0, j], x_r.at[0, j], x_up)
        go(b_piece(x, bz), x_s.at[1, j], x_r.at[1, j], x_dn)

    def pass_x(j, bz):
        arrived(b_piece(x + NX - 1, bz), x_s.at[0, j], x_r.at[0, j])
        go(b_piece(x + NX - 1, bz, 0, half_b), xf_s.at[0, j], xf_r.at[0, j], x_up)
        arrived(b_piece(x + 1, bz), x_s.at[1, j], x_r.at[1, j])
        go(b_piece(x + 1, bz, half_b, half_b), xf_s.at[1, j], xf_r.at[1, j], x_dn)

    def tiles_out():
        def tile_for(owner):
            tile = 0
            for i in range(1, TILES_OWN):
                tile = jnp.where(tile_owner[i] == owner, i, tile)
            return tile

        rbuf[me] = tok[tile_for(me)]

        @pl.loop(1, N_BAL)
        def _(d):
            to = (me + d) % N_BAL
            owner_row(d, to, me).start()
            obuf[to] = tok[tile_for(to)]
            relay(d, to, me).start()

    def tiles_in():
        @pl.loop(1, N_BAL)
        def _(d):
            source = (me + N_BAL - d) % N_BAL
            move(row_own, row_all.at[source], own_s.at[d], own_r.at[d], z_up).wait_recv()

        source_id = lax.broadcasted_iota(jnp.int32, (N_BAL, 128), 0)
        lane = lax.broadcasted_iota(jnp.int32, (N_BAL, 128), 1)
        hits = (row_all[:, 0, :] == me).astype(jnp.int32)
        gives = jnp.broadcast_to(jnp.max(hits, axis=1, keepdims=True), (N_BAL, 128))
        upto = gives
        for shift in (1, 2, 4, 8, 16):
            upto = upto + jnp.where(source_id >= shift, pltpu.roll(upto, shift, 0), 0)
        position = upto - gives
        found = jnp.where((gives > 0) & (position == lane), source_id, 0)
        place[0:N_BAL] = jnp.minimum(position, TILES_OWN - 1)
        place[N_BAL : N_BAL + 8] = jnp.broadcast_to(jnp.sum(found, axis=0, keepdims=True), (8, 128))
        fetch = pltpu.make_async_copy(place, place_s, place_sem)
        fetch.start()
        fetch.wait()

        @pl.loop(1, N_BAL)
        def _(d):
            source = (me + N_BAL - d) % N_BAL
            move(obuf.at[source], rbuf.at[source], rel_s.at[d], rel_r.at[d], z_up).wait_recv()

        @pl.loop(0, TILES_OWN)
        def _(r):
            values = rbuf[place_s[N_BAL, r]].astype(jnp.float32)
            center = jnp.mean(values, axis=-1, keepdims=True)
            away = values - center
            spread = jnp.mean(away * away, axis=-1, keepdims=True)
            clip = jnp.minimum(clip_at(r), MAXCLIPS - 1)
            shift = mod[0, clip, 0:1, :]
            scale = mod[0, clip, 1:2, :]
            normed = away * lax.rsqrt(spread + eps_norm) * (1.0 + scale) + shift
            gbuf[sq, r] = normed.astype(jnp.bfloat16)

        go(piece(y, core), y_s.at[0], y_r.at[0], y_up)
        go(piece(y, core), y_s.at[1], y_r.at[1], y_dn)
        go(piece(y, core), c_s.at[0], c_r.at[0], other)

    def step_z(k):
        if k < NZ // 2:
            size, lo = (ROWS_B, 0) if k < NZ // 2 - 1 else (half_b, half_b)
            arrived(b_piece(x, z + NZ - k), z_s.at[0, k], z_r.at[0, k])
            go(b_piece(x, z + NZ - k, 0, size), z_s.at[0, k + 1], z_r.at[0, k + 1], z_up)
            arrived(b_piece(x, z + k), z_s.at[1, k], z_r.at[1, k])
            go(b_piece(x, z + k, lo, size), z_s.at[1, k + 1], z_r.at[1, k + 1], z_dn)
            send_x(NZ - k, z + NZ - k)
            send_x(k, z + k)
        else:
            arrived(b_piece(x, z + k, 0, half_b), z_s.at[0, k], z_r.at[0, k])
            arrived(b_piece(x, z + k, half_b, half_b), z_s.at[1, k], z_r.at[1, k])
            send_x(k, z + k)

    def a_forward():
        arrived(a_piece(x + NX - 1, z), ax_s.at[0], ax_r.at[0])
        go(a_piece(x + NX - 1, z, 0, half_a), axf_s.at[0], axf_r.at[0], x_up)
        arrived(a_piece(x + 1, z), ax_s.at[1], ax_r.at[1])
        go(a_piece(x + 1, z, half_a, half_a), axf_s.at[1], axf_r.at[1], x_dn)

    def step_az(k):
        if k == 0:
            arrived(a_piece(x + 2, z, 0, half_a), axf_s.at[0], axf_r.at[0])
            arrived(a_piece(x + 2, z, half_a, half_a), axf_s.at[1], axf_r.at[1])
            go(a_block(z), az_s.at[0, 1], az_r.at[0, 1], z_up)
            go(a_block(z), az_s.at[1, 1], az_r.at[1, 1], z_dn)
        elif k < NZ // 2:
            size, lo = (NX, 0) if k < NZ // 2 - 1 else (NX // 2, NX // 2)
            arrived(a_block(z + NZ - k), az_s.at[0, k], az_r.at[0, k])
            go(a_block(z + NZ - k, 0, size), az_s.at[0, k + 1], az_r.at[0, k + 1], z_up)
            arrived(a_block(z + k), az_s.at[1, k], az_r.at[1, k])
            go(a_block(z + k, lo, size), az_s.at[1, k + 1], az_r.at[1, k + 1], z_dn)
        else:
            arrived(a_block(z + k, 0, NX // 2), az_s.at[0, k], az_r.at[0, k])
            arrived(a_block(z + k, NX // 2, NX // 2), az_s.at[1, k], az_r.at[1, k])

    def step_p(j):
        pass_x(j, z + j)
        if j not in (0, NZ // 2):
            pass_x(NZ - j, z + NZ - j)

    def far_x():
        for j in range(NZ):
            arrived(b_piece(x + 2, z + j, 0, half_b), xf_s.at[0, j], xf_r.at[0, j])
            arrived(b_piece(x + 2, z + j, half_b, half_b), xf_s.at[1, j], xf_r.at[1, j])

    def piece(sy, sc, lo=0, size=TILES_OWN):
        return gbuf.at[(sy % NY) * 2 + sc, pl.ds(lo, size)]

    def near_y():
        arrived(piece(y + NY - 1, core), y_s.at[0], y_r.at[0])
        go(piece(y + NY - 1, core, 0, half_t), yf_s.at[0], yf_r.at[0], y_up)
        go(piece(y + NY - 1, core), c_s.at[1], c_r.at[1], other)
        arrived(piece(y + 1, core), y_s.at[1], y_r.at[1])
        go(piece(y + 1, core, half_t, half_t), yf_s.at[1], yf_r.at[1], y_dn)
        go(piece(y + 1, core), c_s.at[2], c_r.at[2], other)

    def far_y():
        arrived(piece(y + 2, core, 0, half_t), yf_s.at[0], yf_r.at[0])
        go(piece(y + 2, core, 0, half_t), c_s.at[3], c_r.at[3], other)
        arrived(piece(y + 2, core, half_t, half_t), yf_s.at[1], yf_r.at[1])
        go(piece(y + 2, core, half_t, half_t), c_s.at[4], c_r.at[4], other)
        arrived(piece(y, 1 - core), c_s.at[0], c_r.at[0])
        arrived(piece(y + NY - 1, 1 - core), c_s.at[1], c_r.at[1])
        arrived(piece(y + 1, 1 - core), c_s.at[2], c_r.at[2])
        arrived(piece(y + 2, 1 - core, 0, half_t), c_s.at[3], c_r.at[3])
        arrived(piece(y + 2, 1 - core, half_t, half_t), c_s.at[4], c_r.at[4])

    go(b_piece(x, z), z_s.at[0, 1], z_r.at[0, 1], z_up)
    go(b_piece(x, z), z_s.at[1, 1], z_r.at[1, 1], z_dn)
    go(a_piece(x, z), ax_s.at[0], ax_r.at[0], x_up)
    go(a_piece(x, z), ax_s.at[1], ax_r.at[1], x_dn)
    for event in ORDER:
        if event == "R0":
            tiles_out()
        elif event == "R":
            tiles_in()
        elif event == "X0":
            send_x(0, z)
        elif event == "AF":
            a_forward()
        elif event == "F":
            far_x()
        elif event == "Y1":
            near_y()
        elif event == "Y2":
            far_y()
        else:
            {"A": step_az, "Z": step_z, "P": step_p}[event[0]](int(event[1]))

    tokens_all = N_SEQ * GROUP

    def left(g):
        return gbuf[:, :, :, g * k_group : (g + 1) * k_group].reshape(tokens_all, k_group)

    for g in range(NX):
        @pl.loop(0, LOCAL_HEADS)
        def _(h, g=g):
            cols = pl.ds(pl.multiple_of(h * WIDTH, HD), 2 * HD)
            right = wbuf[g, :, :, cols].reshape(k_group, 2 * HD)
            product = jnp.dot(left(g), right, preferred_element_type=jnp.float32)
            if g == 0:
                acc[:, cols] = product
            else:
                acc[:, cols] += product

    @pl.loop(0, N_SEQ)
    def _(s):
        lines = pl.ds(pl.multiple_of(s * GROUP, GROUP), GROUP)
        for which in range(2):
            squares = sum(
                jnp.square(acc[lines, h * WIDTH + which * HD : h * WIDTH + (which + 1) * HD])
                for h in range(LOCAL_HEADS)
            )
            line = jnp.sum(squares.T, axis=0, keepdims=True)
            sums[sq, which * 8 : which * 8 + 8, lines] = jnp.broadcast_to(line, (8, GROUP))

    def sum_row(d, to, slot):
        return move(sums.at[sq], sums.at[slot], sum_s.at[d], sum_r.at[d], {"seq": to})

    for d in range(1, N_SEQ):
        sum_row(d, (sq + d) % N_SEQ, sq).start()
    for g in range(NX):
        right = jnp.concatenate(
            [wbuf[g, :, :, h * WIDTH + 2 * HD : (h + 1) * WIDTH].reshape(k_group, HD) for h in range(LOCAL_HEADS)],
            axis=1,
        )
        product = jnp.dot(left(g), right, preferred_element_type=jnp.float32)
        for h in range(LOCAL_HEADS):
            cols = slice(h * WIDTH + 2 * HD, (h + 1) * WIDTH)
            if g == 0:
                acc[:, cols] = product[:, h * HD : (h + 1) * HD]
            else:
                acc[:, cols] += product[:, h * HD : (h + 1) * HD]

    for d in range(1, N_SEQ):
        source = (sq + N_SEQ - d) % N_SEQ
        move(sums.at[source], sums.at[source], sum_s.at[d], sum_r.at[d], z_up).wait_recv()

    @pl.loop(0, N_SEQ)
    def _(s):
        lines = pl.ds(pl.multiple_of(s * GROUP, GROUP), GROUP)
        for which, gain, to in ((0, q_gain, qn), (1, k_gain, kn)):
            line = sum(sums[t, which * 8 : which * 8 + 8, lines] for t in range(N_SEQ))
            scale = lax.rsqrt(line / (HEADS * HD) + eps_norm)
            scale = jnp.broadcast_to(scale[0:1], (HD, GROUP)).T
            for h in range(LOCAL_HEADS):
                raw = acc[lines, h * WIDTH + which * HD : h * WIDTH + (which + 1) * HD]
                to[h, lines] = (raw * scale * gain[h : h + 1]).astype(jnp.bfloat16)
        for h in range(LOCAL_HEADS):
            vn[h, lines] = acc[lines, h * WIDTH + 2 * HD : (h + 1) * WIDTH].astype(jnp.bfloat16)

    def attend(s, ref, slot):
        lines = pl.ds(pl.multiple_of(s * GROUP, GROUP), GROUP)
        for h in range(LOCAL_HEADS):
            scores = lax.dot_general(
                qn[h, lines], kn[h], (((1,), (1,)), ((), ())), preferred_element_type=jnp.float32
            )
            scores = scores * (HD**-0.5 * LOG2_E) + bias[...]
            weights = jnp.exp2(scores - jnp.max(scores, axis=-1, keepdims=True))
            totals = jnp.sum(weights, axis=-1, keepdims=True)
            result = jnp.dot(
                weights.astype(jnp.bfloat16), vn[h], preferred_element_type=jnp.float32
            ) / totals
            ref[slot, :, :, h * HD : (h + 1) * HD] = result.reshape(TILES_OWN, PER, HD).astype(jnp.bfloat16)

    def head_group(d, to, slot):
        return move(att.at[to], heads.at[slot], att_s.at[d], att_r.at[d], {"seq": to})

    @pl.loop(1, N_SEQ)
    def _(d):
        to = (sq + d) % N_SEQ
        attend(to, att, to)
        head_group(d, to, sq).start()

    attend(sq, heads, sq)

    @pl.loop(1, N_SEQ)
    def _(d):
        source = (sq + N_SEQ - d) % N_SEQ
        move(att.at[source], heads.at[source], att_s.at[d], att_r.at[d], z_up).wait_recv()

    part_width = LOCAL_HEADS * HD

    def fill(ref, slot, source):
        tile = place_s[source, 0]
        for s in range(N_SEQ):
            ref[slot, :, s * part_width : (s + 1) * part_width] = heads[s, tile]

    @pl.loop(1, N_BAL)
    def _(d):
        to = (me + d) % N_BAL
        fill(back, to, to)
        back_relay(d, to, me).start()

    fill(came_back, me, me)

    @pl.loop(1, N_BAL)
    def _(d):
        source = (me + N_BAL - d) % N_BAL
        move(back.at[source], came_back.at[source], ret_s.at[d], ret_r.at[d], z_up).wait_recv()

    for i in range(TILES_OWN):
        out[i] = came_back[tile_owner[i]]

    @pl.loop(1, N_BAL)
    def _(d):
        to = (me + d) % N_BAL
        owner_row(d, to, me).wait_send()
        relay(d, to, me).wait_send()
        back_relay(d, to, me).wait_send()

    @pl.loop(1, N_SEQ)
    def _(d):
        to = (sq + d) % N_SEQ
        sum_row(d, to, sq).wait_send()
        head_group(d, to, sq).wait_send()

    for c in started:
        c.wait_send()


def per_device(tokens, w_qkv, q_gain, k_gain, modulation, tile_owner, clip_dims):
    tiles, per, d_model = tokens.shape
    rows = w_qkv.shape[0]
    dma = pltpu.SemaphoreType.DMA
    vmem = pl.BlockSpec(memory_space=pltpu.VMEM)
    smem = pl.BlockSpec(memory_space=pltpu.SMEM)
    m = N_SEQ * GROUP
    columns = LOCAL_HEADS * WIDTH
    bf16, f32, i32 = jnp.bfloat16, jnp.float32, jnp.int32
    call = pl.pallas_call(
        kernel,
        out_shape=jax.ShapeDtypeStruct((tiles, per, HEADS * HD), bf16),
        in_specs=[smem] * 2 + [vmem] * 5,
        out_specs=vmem,
        scratch_shapes=[
            pltpu.VMEM((NX, NZ, rows, columns), bf16),
            pltpu.VMEM((N_SEQ, tiles, per, d_model), bf16),
            pltpu.VMEM((N_BAL, per, d_model), bf16),
            pltpu.VMEM((N_BAL, per, d_model), bf16),
            pltpu.VMEM((m, columns), f32),
            pltpu.VMEM((8, 128), i32),
            pltpu.VMEM((N_BAL, 8, 128), i32),
            pltpu.VMEM((N_BAL + 8, 128), i32),
            pltpu.VMEM((N_SEQ, 16, m), f32),
            pltpu.VMEM((GROUP, m), f32),
            pltpu.VMEM((LOCAL_HEADS, m, HD), bf16),
            pltpu.VMEM((LOCAL_HEADS, m, HD), bf16),
            pltpu.VMEM((LOCAL_HEADS, m, HD), bf16),
            pltpu.VMEM((N_SEQ, tiles, per, LOCAL_HEADS * HD), bf16),
            pltpu.VMEM((N_SEQ, tiles, per, LOCAL_HEADS * HD), bf16),
            pltpu.VMEM((N_BAL, per, HEADS * HD), bf16),
            pltpu.VMEM((N_BAL, per, HEADS * HD), bf16),
            pltpu.SMEM((N_BAL + 8, 128), i32),
            dma((N_BAL,)), dma((N_BAL,)),
            dma((2, 5)), dma((2, 5)),
            dma((2, NZ)), dma((2, NZ)),
            dma((2, NZ)), dma((2, NZ)),
            dma((2,)), dma((2,)), dma((2,)), dma((2,)),
            dma((2, 5)), dma((2, 5)),
            dma((2,)), dma((2,)), dma((2,)), dma((2,)),
            dma((5,)), dma((5,)),
            dma((N_BAL,)), dma((N_BAL,)), dma,
            dma((N_SEQ,)), dma((N_SEQ,)),
            dma((N_SEQ,)), dma((N_SEQ,)),
            dma((N_BAL,)), dma((N_BAL,)),
        ],
        compiler_params=pltpu.CompilerParams(
            collective_id=0, has_side_effects=True, vmem_limit_bytes=58 * 2**20
        ),
        cost_estimate=pl.CostEstimate(
            flops=2 * m * d_model * columns, bytes_accessed=8 * 2**20, transcendentals=0
        ),
        name="relaid_tile_attention",
    )
    return call(
        tile_owner, clip_dims.reshape(-1), tokens, w_qkv.transpose(1, 0, 2), modulation, q_gain, k_gain
    )


def solution(mesh):
    return jax.shard_map(
        per_device,
        mesh=mesh,
        in_specs=(
            P("bal", "seq", None),
            P("bal", "seq", None),
            P("seq", None),
            P("seq", None),
            P("bal", None, None, None),
            P("bal"),
            P("bal", None, None),
        ),
        out_specs=P("bal", "seq", None),
        check_vma=False,
    )
```

time: 317 us -> 214 us (0.68)
  blocking collectives: 98.9 us -> 0 us
  Pallas kernels: 172 us -> 209 us
  matrix products: 21.7 us -> 0 us
  local copies, waits for them, and re-layouts: 17.7 us -> 3.42 us
  other arithmetic: 5.37 us -> 0 us
    all_to_all x2 -> x0, blocking collectives: 59.8 us -> none  [the longest x1 44.1 us: per_device(): lax.all_to_all(spread_back, 'bal', split_axis=0, concat_axis=0, tiled=True)]
    pallas_call x1, Pallas kernels: 172 us -> 209 us  [per_device(): call(tile_owner, clip_dims.reshape(-1), tokens, w_qkv.transpose(1, 0, 2),...]
    unnamed x1 -> x0, blocking collectives: 22.6 us -> none
    psum x1 -> x0, blocking collectives: 16.5 us -> none  [per_device(): lax.psum((jnp.sum(jnp.square(query), axis=(1, 2)), jnp.sum(jnp.square(key...]
    sub x2 -> x0, matrix products: 13.3 us -> none  [attend(): exp_scores = jnp.exp(scores - largest)]
    dot_general x4 -> x0, matrix products: 8.4 us -> none  [the longest x2 7.32 us: attend(): jnp.einsum('hqk,khd->qhd', weights, values, preferred_element_type=jnp.fl...]
    pallas_call x1 -> x0, local copies, waits for them, and re-layouts: 6.06 us -> none  [project(): pl.pallas_call(project_kernel, out_shape=jax.ShapeDtypeStruct((m, heads *...]
    unnamed x24 -> x2, local copies, waits for them, and re-layouts: 8.11 us -> 2.83 us
where the time goes in v2:
time: 214 us; the launch traced here: 212 us
  Pallas kernels  209 us (98%)
  local copies, waits for them, and re-layouts  3.42 us (2%)
    pallas_call x1, Pallas kernels, per_device(): call(tile_owner, clip_dims.reshape(-1), tokens, w_qkv.transpose(1, 0, 2),...  209 us

profile of v2, /device:TPU:32, one launch (start us, length us, event | category | flops | bytes accessed | tf_op | source)
XLA Modules:
  0.0 212.3 jit_solution(10145152977461390450)
XLA Ops:
  0.0 0.8 copy.9
  0.8 0.6 reshape.3.clip_dims
  1.4 208.8 %relaid_tile_attention.1 = bf16[16,8,3072]{2,1,0:T(8,128)(2,1)} custom-call(s32[16]{0:T(128)} %tile_owner.1, s32[12]{0:T(128)} %reshape.3.clip_dims, bf16[16,8,5120]{2,1,0:T(8,128)(2,1)} %tok.1, bf16[3,160,384]{2,1,0:T(8,128)(2,1)} %bitcast.1, f32[1,4,2,5120]{3,2,1,0:T(2,128)} %mod.1, f32[3,128]{1,0:T(4,128)} %q_gain.1, f32[3,128]{1,0:T(4,128)} %k_gain.1), custom_call_target="tpu_custom_call" | custom-call | flops 12079595520 | bytes 8388608 | tf_op jit(solution)/shard_map/relaid_tile_attention/pallas_call | solution.py:488
  210.2 2.1 copy.11

commit v3 on v2

--- a/solution.py
+++ b/solution.py
@@ -14,10 +14,15 @@
 MAXCLIPS = 4
 PER = 8
 GROUP = TILES_OWN * PER
+HALF = PER // 2
+PAIRS = TILES_OWN // 2
 LOCAL_HEADS = HEADS // N_SEQ
 WIDTH = 3 * HD
 ROWS_B = 128
-ORDER = ("R0", "X0", "AF", "Z1", "A0", "P0", "P1", "R", "Z2", "A1", "Z3", "P2", "A2", "Z4", "P3", "A3", "Y1", "P4", "A4", "F", "Y2")
+ORDER = (
+    "R0", "X0", "AF", "Z1", "A0", "P0", "P1", "Z2", "R1", "Y1", "A1", "Z3", "P2", "R2", "Z4", "A2", "P3", "A3", "Y2", "P4", "A4",
+    "F1", "F2", "M1", "F", "M2",
+)
 
 eps_norm = 1e-06
 score_fill = -1e30
@@ -27,7 +32,7 @@
 
 def kernel(
     tile_owner, clip_dims, tok, w_in, mod, q_gain, k_gain, out,
-    wbuf, gbuf, obuf, rbuf, acc, row_own, row_all, place, sums, bias, qn, kn, vn, att, heads, back, came_back, place_s,
+    wbuf, gbuf, halves, mods, obuf, rbuf_1, rbuf_2, acc, row_own, row_all, place, sums, bias, qn, kn, vn, att, heads_1, heads_2, heads_3, back, came_1, came_2, came_3, place_s,
     rel_s, rel_r, z_s, z_r, x_s, x_r, xf_s, xf_r, ax_s, ax_r, axf_s, axf_r, az_s, az_r,
     y_s, y_r, yf_s, yf_r, c_s, c_r, own_s, own_r, place_sem, sum_s, sum_r, att_s, att_r, ret_s, ret_r,
 ):
@@ -40,7 +45,10 @@
     rows = w_in.shape[1]
     half_b = ROWS_B // 2
     half_a = (rows - ROWS_B) // 2
-    half_t = TILES_OWN // 2
+    half_d = d_model // 2
+    rbuf = (rbuf_1, rbuf_2)
+    heads = (heads_1, heads_2, heads_3)
+    came_back = (came_1, came_2, came_3)
 
     def bal(bx, bz):
         return {"bal": (bx % NX) * NZ + bz % NZ}
@@ -112,8 +120,8 @@
         row = (offset >= width).astype(jnp.int32) + (offset >= 2 * width).astype(jnp.int32)
         return member, frame, row, offset - row * width
 
-    of_query = layout(lax.broadcasted_iota(jnp.int32, (GROUP, GROUP), 0) // PER)
-    of_key = layout(lax.broadcasted_iota(jnp.int32, (GROUP, GROUP), 1) // PER)
+    of_query = layout(lax.broadcasted_iota(jnp.int32, (GROUP, GROUP), 0) % (GROUP // 2) // HALF)
+    of_key = layout(lax.broadcasted_iota(jnp.int32, (GROUP, GROUP), 1) % (GROUP // 2) // HALF)
     allowed = of_query[0] == of_key[0]
     for a, b in zip(of_query[1:], of_key[1:], strict=True):
         allowed = allowed & (jnp.abs(a - b) <= 1)
@@ -121,6 +129,22 @@
     for s in range(N_SEQ):
         bias[:, s * GROUP : (s + 1) * GROUP] = bias_tile
 
+    upper = lax.broadcasted_iota(jnp.int32, (8, half_d), 0) < HALF
+
+    def interleave(a, b):
+        return jnp.where(upper, a, pltpu.roll(b, HALF, 0)), jnp.where(upper, pltpu.roll(a, HALF, 0), b)
+
+    @pl.loop(0, TILES_OWN)
+    def _(i):
+        values = tok[i].astype(jnp.float32)
+        for t, half in enumerate(interleave(values[:, :half_d], values[:, half_d:])):
+            halves[t, i] = half.astype(jnp.bfloat16)
+
+    for k in range(MAXCLIPS):
+        for which in range(2):
+            line = mod[0, k, which : which + 1, :]
+            mods[k, which] = jnp.where(upper, line[:, :half_d], line[:, half_d:]) + float(which)
+
     pl.semaphore_wait(barrier, N_BAL + N_SEQ - 2)
 
     def b_piece(bx, bz, lo=0, size=ROWS_B):
@@ -135,11 +159,11 @@
     def owner_row(d, to, slot):
         return move(row_own, row_all.at[slot], own_s.at[d], own_r.at[d], {"bal": to})
 
-    def relay(d, to, slot):
-        return move(obuf.at[to], rbuf.at[slot], rel_s.at[d], rel_r.at[d], {"bal": to})
-
-    def back_relay(d, to, slot):
-        return move(back.at[to], came_back.at[slot], ret_s.at[d], ret_r.at[d], {"bal": to})
+    def relay(t, d, to, slot):
+        return move(obuf.at[t, to], rbuf[t].at[slot], rel_s.at[t, d], rel_r.at[t, d], {"bal": to})
+
+    def back_relay(h, d, to, slot):
+        return move(back.at[h, to], came_back[h].at[slot], ret_s.at[h, d], ret_r.at[h, d], {"bal": to})
 
     def send_x(j, bz):
         go(b_piece(x, bz), x_s.at[0, j], x_r.at[0, j], x_up)
@@ -158,16 +182,20 @@
                 tile = jnp.where(tile_owner[i] == owner, i, tile)
             return tile
 
-        rbuf[me] = tok[tile_for(me)]
+        mine = tile_for(me)
+        for t in range(2):
+            rbuf[t][me] = halves[t, mine]
 
         @pl.loop(1, N_BAL)
         def _(d):
             to = (me + d) % N_BAL
             owner_row(d, to, me).start()
-            obuf[to] = tok[tile_for(to)]
-            relay(d, to, me).start()
-
-    def tiles_in():
+            tile = tile_for(to)
+            obuf[0, to] = halves[0, tile]
+            relay(0, d, to, me).start()
+            obuf[1, to] = halves[1, tile]
+
+    def find_sources():
         @pl.loop(1, N_BAL)
         def _(d):
             source = (me + N_BAL - d) % N_BAL
@@ -188,26 +216,38 @@
         fetch.start()
         fetch.wait()
 
+    def tiles_in(t):
         @pl.loop(1, N_BAL)
         def _(d):
             source = (me + N_BAL - d) % N_BAL
-            move(obuf.at[source], rbuf.at[source], rel_s.at[d], rel_r.at[d], z_up).wait_recv()
-
-        @pl.loop(0, TILES_OWN)
-        def _(r):
-            values = rbuf[place_s[N_BAL, r]].astype(jnp.float32)
-            center = jnp.mean(values, axis=-1, keepdims=True)
-            away = values - center
-            spread = jnp.mean(away * away, axis=-1, keepdims=True)
+            move(obuf.at[t, source], rbuf[t].at[source], rel_s.at[t, d], rel_r.at[t, d], z_up).wait_recv()
+
+        if t == 0:
+            @pl.loop(1, N_BAL)
+            def _(d):
+                relay(1, d, (me + d) % N_BAL, me).start()
+
+        def over_features(values):
+            line = jnp.sum(values, axis=-1, keepdims=True)
+            line = jnp.broadcast_to(line, (8, 128))
+            return ((line + pltpu.roll(line, HALF, 0)) * (1.0 / d_model))[:, 0:1]
+
+        def normed(r):
+            values = rbuf[t][place_s[N_BAL, r]].astype(jnp.float32)
+            away = values - over_features(values)
+            spread = over_features(away * away)
             clip = jnp.minimum(clip_at(r), MAXCLIPS - 1)
-            shift = mod[0, clip, 0:1, :]
-            scale = mod[0, clip, 1:2, :]
-            normed = away * lax.rsqrt(spread + eps_norm) * (1.0 + scale) + shift
-            gbuf[sq, r] = normed.astype(jnp.bfloat16)
-
-        go(piece(y, core), y_s.at[0], y_r.at[0], y_up)
-        go(piece(y, core), y_s.at[1], y_r.at[1], y_dn)
-        go(piece(y, core), c_s.at[0], c_r.at[0], other)
+            return away * lax.rsqrt(spread + eps_norm) * mods[clip, 1] + mods[clip, 0]
+
+        @pl.loop(0, PAIRS)
+        def _(p):
+            low, high = interleave(normed(2 * p), normed(2 * p + 1))
+            gbuf[sq, t, p, :, :half_d] = low.astype(jnp.bfloat16)
+            gbuf[sq, t, p, :, half_d:] = high.astype(jnp.bfloat16)
+
+        go(piece(t, y, core), y_s.at[0, t], y_r.at[0, t], y_up)
+        go(piece(t, y, core), y_s.at[1, t], y_r.at[1, t], y_dn)
+        go(piece(t, y, core), c_s.at[0, t], c_r.at[0, t], other)
 
     def step_z(k):
         if k < NZ // 2:
@@ -255,27 +295,60 @@
             arrived(b_piece(x + 2, z + j, 0, half_b), xf_s.at[0, j], xf_r.at[0, j])
             arrived(b_piece(x + 2, z + j, half_b, half_b), xf_s.at[1, j], xf_r.at[1, j])
 
-    def piece(sy, sc, lo=0, size=TILES_OWN):
-        return gbuf.at[(sy % NY) * 2 + sc, pl.ds(lo, size)]
-
-    def near_y():
-        arrived(piece(y + NY - 1, core), y_s.at[0], y_r.at[0])
-        go(piece(y + NY - 1, core, 0, half_t), yf_s.at[0], yf_r.at[0], y_up)
-        go(piece(y + NY - 1, core), c_s.at[1], c_r.at[1], other)
-        arrived(piece(y + 1, core), y_s.at[1], y_r.at[1])
-        go(piece(y + 1, core, half_t, half_t), yf_s.at[1], yf_r.at[1], y_dn)
-        go(piece(y + 1, core), c_s.at[2], c_r.at[2], other)
-
-    def far_y():
-        arrived(piece(y + 2, core, 0, half_t), yf_s.at[0], yf_r.at[0])
-        go(piece(y + 2, core, 0, half_t), c_s.at[3], c_r.at[3], other)
-        arrived(piece(y + 2, core, half_t, half_t), yf_s.at[1], yf_r.at[1])
-        go(piece(y + 2, core, half_t, half_t), c_s.at[4], c_r.at[4], other)
-        arrived(piece(y, 1 - core), c_s.at[0], c_r.at[0])
-        arrived(piece(y + NY - 1, 1 - core), c_s.at[1], c_r.at[1])
-        arrived(piece(y + 1, 1 - core), c_s.at[2], c_r.at[2])
-        arrived(piece(y + 2, 1 - core, 0, half_t), c_s.at[3], c_r.at[3])
-        arrived(piece(y + 2, 1 - core, half_t, half_t), c_s.at[4], c_r.at[4])
+    half_p = PAIRS // 2
+
+    def piece(t, sy, sc, lo=0, size=PAIRS):
+        return gbuf.at[(sy % NY) * 2 + sc, t, pl.ds(lo, size)]
+
+    def near_y(t):
+        for way, (frm, to) in enumerate(((y + NY - 1, y_up), (y + 1, y_dn))):
+            arrived(piece(t, frm, core), y_s.at[way, t], y_r.at[way, t])
+            go(piece(t, frm, core, way * half_p, half_p), yf_s.at[way, t], yf_r.at[way, t], to)
+            go(piece(t, frm, core), c_s.at[1 + way, t], c_r.at[1 + way, t], other)
+
+    def far_y(t):
+        for way in range(2):
+            far = piece(t, y + 2, core, way * half_p, half_p)
+            arrived(far, yf_s.at[way, t], yf_r.at[way, t])
+            go(far, c_s.at[3 + way, t], c_r.at[3 + way, t], other)
+        arrived(piece(t, y, 1 - core), c_s.at[0, t], c_r.at[0, t])
+        for way, frm in enumerate((y + NY - 1, y + 1)):
+            arrived(piece(t, frm, 1 - core), c_s.at[1 + way, t], c_r.at[1 + way, t])
+            arrived(piece(t, y + 2, 1 - core, way * half_p, half_p), c_s.at[3 + way, t], c_r.at[3 + way, t])
+
+    tokens_all = N_SEQ * GROUP
+
+    def left(g):
+        columns = pl.ds(pl.multiple_of(g * k_group, 128), k_group)
+        return gbuf[:, :, :, :, columns].reshape(tokens_all, k_group)
+
+    def project_qk(g, first):
+        @pl.loop(0, LOCAL_HEADS)
+        def _(h):
+            cols = pl.ds(pl.multiple_of(h * WIDTH, HD), 2 * HD)
+            right = wbuf[g, :, :, cols].reshape(k_group, 2 * HD)
+            product = jnp.dot(left(g), right, preferred_element_type=jnp.float32)
+            if first:
+                acc[:, cols] = product
+            else:
+                acc[:, cols] += product
+
+    def project_v(g, first):
+        right = jnp.concatenate(
+            [wbuf[g, :, :, h * WIDTH + 2 * HD : (h + 1) * WIDTH].reshape(k_group, HD) for h in range(LOCAL_HEADS)],
+            axis=1,
+        )
+        product = jnp.dot(left(g), right, preferred_element_type=jnp.float32)
+        for h in range(LOCAL_HEADS):
+            cols = slice(h * WIDTH + 2 * HD, (h + 1) * WIDTH)
+            if first:
+                acc[:, cols] = product[:, h * HD : (h + 1) * HD]
+            else:
+                acc[:, cols] += product[:, h * HD : (h + 1) * HD]
+
+    def project_near():
+        for i, step in enumerate((0, 1, NX - 1)):
+            project_qk((x + step) % NX, i == 0)
 
     go(b_piece(x, z), z_s.at[0, 1], z_r.at[0, 1], z_up)
     go(b_piece(x, z), z_s.at[1, 1], z_r.at[1, 1], z_dn)
@@ -284,36 +357,29 @@
     for event in ORDER:
         if event == "R0":
             tiles_out()
-        elif event == "R":
-            tiles_in()
+        elif event == "R1":
+            find_sources()
+            tiles_in(0)
+        elif event == "R2":
+            tiles_in(1)
         elif event == "X0":
             send_x(0, z)
         elif event == "AF":
             a_forward()
         elif event == "F":
             far_x()
-        elif event == "Y1":
-            near_y()
-        elif event == "Y2":
-            far_y()
+        elif event == "M1":
+            project_near()
+        elif event == "M2":
+            project_qk((x + 2) % NX, False)
         else:
-            {"A": step_az, "Z": step_z, "P": step_p}[event[0]](int(event[1]))
-
-    tokens_all = N_SEQ * GROUP
-
-    def left(g):
-        return gbuf[:, :, :, g * k_group : (g + 1) * k_group].reshape(tokens_all, k_group)
-
-    for g in range(NX):
-        @pl.loop(0, LOCAL_HEADS)
-        def _(h, g=g):
-            cols = pl.ds(pl.multiple_of(h * WIDTH, HD), 2 * HD)
-            right = wbuf[g, :, :, cols].reshape(k_group, 2 * HD)
-            product = jnp.dot(left(g), right, preferred_element_type=jnp.float32)
-            if g == 0:
-                acc[:, cols] = product
+            number = int(event[1])
+            if event[0] == "Y":
+                near_y(number - 1)
+            elif event[0] == "F":
+                far_y(number - 1)
             else:
-                acc[:, cols] += product
+                {"A": step_az, "Z": step_z, "P": step_p}[event[0]](number)
 
     @pl.loop(0, N_SEQ)
     def _(s):
@@ -331,18 +397,8 @@
 
     for d in range(1, N_SEQ):
         sum_row(d, (sq + d) % N_SEQ, sq).start()
-    for g in range(NX):
-        right = jnp.concatenate(
-            [wbuf[g, :, :, h * WIDTH + 2 * HD : (h + 1) * WIDTH].reshape(k_group, HD) for h in range(LOCAL_HEADS)],
-            axis=1,
-        )
-        product = jnp.dot(left(g), right, preferred_element_type=jnp.float32)
-        for h in range(LOCAL_HEADS):
-            cols = slice(h * WIDTH + 2 * HD, (h + 1) * WIDTH)
-            if g == 0:
-                acc[:, cols] = product[:, h * HD : (h + 1) * HD]
-            else:
-                acc[:, cols] += product[:, h * HD : (h + 1) * HD]
+    for i, step in enumerate((0, 1, NX - 1, 2)):
+        project_v((x + step) % NX, i == 0)
 
     for d in range(1, N_SEQ):
         source = (sq + N_SEQ - d) % N_SEQ
@@ -361,71 +417,87 @@
         for h in range(LOCAL_HEADS):
             vn[h, lines] = acc[lines, h * WIDTH + 2 * HD : (h + 1) * WIDTH].astype(jnp.bfloat16)
 
-    def attend(s, ref, slot):
+    def attend(h, s):
         lines = pl.ds(pl.multiple_of(s * GROUP, GROUP), GROUP)
-        for h in range(LOCAL_HEADS):
-            scores = lax.dot_general(
-                qn[h, lines], kn[h], (((1,), (1,)), ((), ())), preferred_element_type=jnp.float32
-            )
-            scores = scores * (HD**-0.5 * LOG2_E) + bias[...]
-            weights = jnp.exp2(scores - jnp.max(scores, axis=-1, keepdims=True))
-            totals = jnp.sum(weights, axis=-1, keepdims=True)
-            result = jnp.dot(
-                weights.astype(jnp.bfloat16), vn[h], preferred_element_type=jnp.float32
-            ) / totals
-            ref[slot, :, :, h * HD : (h + 1) * HD] = result.reshape(TILES_OWN, PER, HD).astype(jnp.bfloat16)
-
-    def head_group(d, to, slot):
-        return move(att.at[to], heads.at[slot], att_s.at[d], att_r.at[d], {"seq": to})
-
-    @pl.loop(1, N_SEQ)
-    def _(d):
-        to = (sq + d) % N_SEQ
-        attend(to, att, to)
-        head_group(d, to, sq).start()
-
-    attend(sq, heads, sq)
-
-    @pl.loop(1, N_SEQ)
-    def _(d):
-        source = (sq + N_SEQ - d) % N_SEQ
-        move(att.at[source], heads.at[source], att_s.at[d], att_r.at[d], z_up).wait_recv()
-
-    part_width = LOCAL_HEADS * HD
-
-    def fill(ref, slot, source):
-        tile = place_s[source, 0]
+        scores = lax.dot_general(
+            qn[h, lines], kn[h], (((1,), (1,)), ((), ())), preferred_element_type=jnp.float32
+        )
+        scores = scores * (HD**-0.5 * LOG2_E) + bias[...]
+        weights = jnp.exp2(scores - jnp.max(scores, axis=-1, keepdims=True))
+        totals = jnp.sum(weights, axis=-1, keepdims=True)
+        result = jnp.dot(
+            weights.astype(jnp.bfloat16), vn[h], preferred_element_type=jnp.float32
+        ) / totals
+        result = result.reshape(2, PAIRS, 8, HD)
+        first, second = result[0], result[1]
+        top = lax.broadcasted_iota(jnp.int32, (PAIRS, 8, HD), 1) < HALF
+        even = jnp.where(top, first, pltpu.roll(second, HALF, 1))
+        odd = jnp.where(top, pltpu.roll(first, HALF, 1), second)
+        return jnp.stack([even, odd], axis=1).reshape(TILES_OWN, PER, HD).astype(jnp.bfloat16)
+
+    def head_group(h, d, to, slot):
+        return move(att.at[h, to], heads[h].at[slot], att_s.at[h, d], att_r.at[h, d], {"seq": to})
+
+    def attend_all(h):
+        @pl.loop(1, N_SEQ)
+        def _(d):
+            to = (sq + d) % N_SEQ
+            att[h, to] = attend(h, to)
+            head_group(h, d, to, sq).start()
+
+        heads[h][sq] = attend(h, sq)
+
+    def send_back(h):
+        @pl.loop(1, N_SEQ)
+        def _(d):
+            source = (sq + N_SEQ - d) % N_SEQ
+            move(att.at[h, source], heads[h].at[source], att_s.at[h, d], att_r.at[h, d], z_up).wait_recv()
+
+        @pl.loop(1, N_BAL)
+        def _(d):
+            to = (me + d) % N_BAL
+            tile = place_s[to, 0]
+            for s in range(N_SEQ):
+                back[h, to, :, s * HD : (s + 1) * HD] = heads[h][s, tile]
+            back_relay(h, d, to, me).start()
+
+        tile = place_s[me, 0]
         for s in range(N_SEQ):
-            ref[slot, :, s * part_width : (s + 1) * part_width] = heads[s, tile]
-
-    @pl.loop(1, N_BAL)
-    def _(d):
-        to = (me + d) % N_BAL
-        fill(back, to, to)
-        back_relay(d, to, me).start()
-
-    fill(came_back, me, me)
-
-    @pl.loop(1, N_BAL)
-    def _(d):
-        source = (me + N_BAL - d) % N_BAL
-        move(back.at[source], came_back.at[source], ret_s.at[d], ret_r.at[d], z_up).wait_recv()
-
-    for i in range(TILES_OWN):
-        out[i] = came_back[tile_owner[i]]
+            came_back[h][me, :, s * HD : (s + 1) * HD] = heads[h][s, tile]
+
+    for h in range(LOCAL_HEADS):
+        attend_all(h)
+        if h:
+            send_back(h - 1)
+    send_back(LOCAL_HEADS - 1)
+
+    for h in range(LOCAL_HEADS):
+        @pl.loop(1, N_BAL)
+        def _(d, h=h):
+            source = (me + N_BAL - d) % N_BAL
+            move(back.at[h, source], came_back[h].at[source], ret_s.at[h, d], ret_r.at[h, d], z_up).wait_recv()
+
+        for i in range(TILES_OWN):
+            tile = came_back[h][tile_owner[i]]
+            for s in range(N_SEQ):
+                column = (s * LOCAL_HEADS + h) * HD
+                out[i, :, column : column + HD] = tile[:, s * HD : (s + 1) * HD]
 
     @pl.loop(1, N_BAL)
     def _(d):
         to = (me + d) % N_BAL
         owner_row(d, to, me).wait_send()
-        relay(d, to, me).wait_send()
-        back_relay(d, to, me).wait_send()
+        relay(0, d, to, me).wait_send()
+        relay(1, d, to, me).wait_send()
+        for h in range(LOCAL_HEADS):
+            back_relay(h, d, to, me).wait_send()
 
     @pl.loop(1, N_SEQ)
     def _(d):
         to = (sq + d) % N_SEQ
         sum_row(d, to, sq).wait_send()
-        head_group(d, to, sq).wait_send()
+        for h in range(LOCAL_HEADS):
+            head_group(h, d, to, sq).wait_send()
 
     for c in started:
         c.wait_send()
@@ -447,9 +519,12 @@
         out_specs=vmem,
         scratch_shapes=[
             pltpu.VMEM((NX, NZ, rows, columns), bf16),
-            pltpu.VMEM((N_SEQ, tiles, per, d_model), bf16),
-            pltpu.VMEM((N_BAL, per, d_model), bf16),
-            pltpu.VMEM((N_BAL, per, d_model), bf16),
+            pltpu.VMEM((N_SEQ, 2, PAIRS, 8, d_model), bf16),
+            pltpu.VMEM((2, tiles, 8, d_model // 2), bf16),
+            pltpu.VMEM((MAXCLIPS, 2, 8, d_model // 2), f32),
+            pltpu.VMEM((2, N_BAL, 8, d_model // 2), bf16),
+            pltpu.VMEM((N_BAL, 8, d_model // 2), bf16),
+            pltpu.VMEM((N_BAL, 8, d_model // 2), bf16),
             pltpu.VMEM((m, columns), f32),
             pltpu.VMEM((8, 128), i32),
             pltpu.VMEM((N_BAL, 8, 128), i32),
@@ -459,23 +534,23 @@
             pltpu.VMEM((LOCAL_HEADS, m, HD), bf16),
             pltpu.VMEM((LOCAL_HEADS, m, HD), bf16),
             pltpu.VMEM((LOCAL_HEADS, m, HD), bf16),
-            pltpu.VMEM((N_SEQ, tiles, per, LOCAL_HEADS * HD), bf16),
-            pltpu.VMEM((N_SEQ, tiles, per, LOCAL_HEADS * HD), bf16),
-            pltpu.VMEM((N_BAL, per, HEADS * HD), bf16),
-            pltpu.VMEM((N_BAL, per, HEADS * HD), bf16),
+            pltpu.VMEM((LOCAL_HEADS, N_SEQ, tiles, per, HD), bf16),
+            *[pltpu.VMEM((N_SEQ, tiles, per, HD), bf16)] * LOCAL_HEADS,
+            pltpu.VMEM((LOCAL_HEADS, N_BAL, per, N_SEQ * HD), bf16),
+            *[pltpu.VMEM((N_BAL, per, N_SEQ * HD), bf16)] * LOCAL_HEADS,
             pltpu.SMEM((N_BAL + 8, 128), i32),
-            dma((N_BAL,)), dma((N_BAL,)),
+            dma((2, N_BAL)), dma((2, N_BAL)),
             dma((2, 5)), dma((2, 5)),
             dma((2, NZ)), dma((2, NZ)),
             dma((2, NZ)), dma((2, NZ)),
             dma((2,)), dma((2,)), dma((2,)), dma((2,)),
             dma((2, 5)), dma((2, 5)),
-            dma((2,)), dma((2,)), dma((2,)), dma((2,)),
-            dma((5,)), dma((5,)),
+            dma((2, 2)), dma((2, 2)), dma((2, 2)), dma((2, 2)),
+            dma((5, 2)), dma((5, 2)),
             dma((N_BAL,)), dma((N_BAL,)), dma,
             dma((N_SEQ,)), dma((N_SEQ,)),
-            dma((N_SEQ,)), dma((N_SEQ,)),
-            dma((N_BAL,)), dma((N_BAL,)),
+            dma((LOCAL_HEADS, N_SEQ)), dma((LOCAL_HEADS, N_SEQ)),
+            dma((LOCAL_HEADS, N_BAL)), dma((LOCAL_HEADS, N_BAL)),
         ],
         compiler_params=pltpu.CompilerParams(
             collective_id=0, has_side_effects=True, vmem_limit_bytes=58 * 2**20

time: 214 us -> 202 us (0.944)
  Pallas kernels: 209 us -> 196 us
    pallas_call x1, Pallas kernels: 209 us -> 196 us  [per_device(): call(tile_owner, clip_dims.reshape(-1), tokens, w_qkv.transpose(1, 0, 2),...]
where the time goes in v3:
time: 202 us; the launch traced here: 200 us
  Pallas kernels  196 us (97%)
  local copies, waits for them, and re-layouts  3.42 us (2%)
    pallas_call x1, Pallas kernels, per_device(): call(tile_owner, clip_dims.reshape(-1), tokens, w_qkv.transpose(1, 0, 2),...  196 us

profile of v3, /device:TPU:32, one launch (start us, length us, event | category | flops | bytes accessed | tf_op | source)
XLA Modules:
  0.0 199.7 jit_solution(14032449919255691446)
XLA Ops:
  0.0 0.8 copy.9
  0.8 0.6 reshape.3.clip_dims
  1.4 196.3 %relaid_tile_attention.1 = bf16[16,8,3072]{2,1,0:T(8,128)(2,1)} custom-call(s32[16]{0:T(128)} %tile_owner.1, s32[12]{0:T(128)} %reshape.3.clip_dims, bf16[16,8,5120]{2,1,0:T(8,128)(2,1)} %tok.1, bf16[3,160,384]{2,1,0:T(8,128)(2,1)} %bitcast.1, f32[1,4,2,5120]{3,2,1,0:T(2,128)} %mod.1, f32[3,128]{1,0:T(4,128)} %q_gain.1, f32[3,128]{1,0:T(4,128)} %k_gain.1), custom_call_target="tpu_custom_call" | custom-call | flops 12079595520 | bytes 8388608 | tf_op jit(solution)/shard_map/relaid_tile_attention/pallas_call | solution.py:563
  197.7 2.1 %copy.11 = bf16[16,8,3072]{2,1,0:T(8,128)(2,1)} copy(bf16[16,8,3072]{2,1,0:T(8,128)(2,1)} %relaid_tile_attention.1) | data formatting | bytes 1572864

commit v4 on v3

--- a/solution.py
+++ b/solution.py
@@ -120,15 +120,6 @@
         row = (offset >= width).astype(jnp.int32) + (offset >= 2 * width).astype(jnp.int32)
         return member, frame, row, offset - row * width
 
-    of_query = layout(lax.broadcasted_iota(jnp.int32, (GROUP, GROUP), 0) % (GROUP // 2) // HALF)
-    of_key = layout(lax.broadcasted_iota(jnp.int32, (GROUP, GROUP), 1) % (GROUP // 2) // HALF)
-    allowed = of_query[0] == of_key[0]
-    for a, b in zip(of_query[1:], of_key[1:], strict=True):
-        allowed = allowed & (jnp.abs(a - b) <= 1)
-    bias_tile = jnp.where(allowed, 0.0, score_fill)
-    for s in range(N_SEQ):
-        bias[:, s * GROUP : (s + 1) * GROUP] = bias_tile
-
     upper = lax.broadcasted_iota(jnp.int32, (8, half_d), 0) < HALF
 
     def interleave(a, b):
@@ -140,10 +131,20 @@
         for t, half in enumerate(interleave(values[:, :half_d], values[:, half_d:])):
             halves[t, i] = half.astype(jnp.bfloat16)
 
-    for k in range(MAXCLIPS):
-        for which in range(2):
-            line = mod[0, k, which : which + 1, :]
-            mods[k, which] = jnp.where(upper, line[:, :half_d], line[:, half_d:]) + float(which)
+    def tables():
+        of_query = layout(lax.broadcasted_iota(jnp.int32, (GROUP, GROUP), 0) % (GROUP // 2) // HALF)
+        of_key = layout(lax.broadcasted_iota(jnp.int32, (GROUP, GROUP), 1) % (GROUP // 2) // HALF)
+        allowed = of_query[0] == of_key[0]
+        for a, b in zip(of_query[1:], of_key[1:], strict=True):
+            allowed = allowed & (jnp.abs(a - b) <= 1)
+        bias_tile = jnp.where(allowed, 0.0, score_fill)
+        for s in range(N_SEQ):
+            bias[:, s * GROUP : (s + 1) * GROUP] = bias_tile
+
+        for k in range(MAXCLIPS):
+            for which in range(2):
+                line = mod[0, k, which : which + 1, :]
+                mods[k, which] = jnp.where(upper, line[:, :half_d], line[:, half_d:]) + float(which)
 
     pl.semaphore_wait(barrier, N_BAL + N_SEQ - 2)
 
@@ -357,6 +358,7 @@
     for event in ORDER:
         if event == "R0":
             tiles_out()
+            tables()
         elif event == "R1":
             find_sources()
             tiles_in(0)

time: 202 us -> 202 us (level)
  no operation moved by 1% of the time
where the time goes in v4:
time: 202 us; the launch traced here: 200 us
  Pallas kernels  196 us (97%)
  local copies, waits for them, and re-layouts  3.42 us (2%)
    pallas_call x1, Pallas kernels, per_device(): call(tile_owner, clip_dims.reshape(-1), tokens, w_qkv.transpose(1, 0, 2),...  196 us

profile of v4, /device:TPU:32, one launch (start us, length us, event | category | flops | bytes accessed | tf_op | source)
XLA Modules:
  0.0 199.8 jit_solution(7378980253953683125)
XLA Ops:
  0.0 0.8 copy.9
  0.8 0.6 reshape.3.clip_dims
  1.4 196.3 %relaid_tile_attention.1 = bf16[16,8,3072]{2,1,0:T(8,128)(2,1)} custom-call(s32[16]{0:T(128)} %tile_owner.1, s32[12]{0:T(128)} %reshape.3.clip_dims, bf16[16,8,5120]{2,1,0:T(8,128)(2,1)} %tok.1, bf16[3,160,384]{2,1,0:T(8,128)(2,1)} %bitcast.1, f32[1,4,2,5120]{3,2,1,0:T(2,128)} %mod.1, f32[3,128]{1,0:T(4,128)} %q_gain.1, f32[3,128]{1,0:T(4,128)} %k_gain.1), custom_call_target="tpu_custom_call" | custom-call | flops 12079595520 | bytes 8388608 | tf_op jit(solution)/shard_map/relaid_tile_attention/pallas_call | solution.py:565
  197.7 2.1 %copy.11 = bf16[16,8,3072]{2,1,0:T(8,128)(2,1)} copy(bf16[16,8,3072]{2,1,0:T(8,128)(2,1)} %relaid_tile_attention.1) | data formatting | bytes 1572864
